TPU v7x, 32 devices: a whole 2x2x4 slice. The times are simulated.
32 devices in a mesh: dp: 8 (over z, core), tensor: 4 (over y, x).
Axes of the slice: x: 2, y: 2, z: 4, core: 2. Of those that a mesh axis runs over, the one named last changes fastest.
Arguments:
- hidden_in: bfloat16 [16384, 2048], P(('dp', 'tensor')), may hold values from -6 to 6
- grad_out: bfloat16 [16384, 2048], P(('dp', 'tensor')), may hold values from -6 to 6
- lengths: int32 [16], replicated, may hold values from 256 to 1792, as said below
- owners: int32 [16], replicated, may hold values from 0 to 7, as said below
- qkv_weight: float32 [3, 2048, 2048], P(None, 'dp', 'tensor'), may hold values from -0.125 to 0.125
- out_weight: float32 [2048, 2048], P('tensor', 'dp'), may hold values from -0.5 to 0.5
- gate_up_weight: float32 [2, 2048, 5632], P(None, 'dp', 'tensor'), may hold values from -0.125 to 0.125
- down_weight: float32 [5632, 2048], P('tensor', 'dp'), may hold values from -0.078125 to 0.078125
- norm_gain: float32 [2, 2048], replicated, may hold values from 0.5 to 1.5
- norm_bias: float32 [2, 2048], replicated, may hold values from -1 to 1
- qkv_bias: float32 [3, 2048], replicated, may hold values from -1.5 to 1.5
- qkv_first: float32 [3, 2048, 2048], P(None, 'dp', 'tensor'), may hold values from -8.96 to 8.96
- out_first: float32 [2048, 2048], P('tensor', 'dp'), may hold values from -12.8 to 12.8
- gate_up_first: float32 [2, 2048, 5632], P(None, 'dp', 'tensor'), may hold values from -21.76 to 21.76
- down_first: float32 [5632, 2048], P('tensor', 'dp'), may hold values from -21.76 to 21.76
- small_first: float32 [7, 2048], replicated, may hold values from -21.76 to 21.76
- qkv_second: float32 [3, 2048, 2048], P(None, 'dp', 'tensor'), may hold values from 0.2048 to 3.2768
- out_second: float32 [2048, 2048], P('tensor', 'dp'), may hold values from 0.458752 to 7.3728
- gate_up_second: float32 [2, 2048, 5632], P(None, 'dp', 'tensor'), may hold values from 1.277952 to 20.48
- down_second: float32 [5632, 2048], P('tensor', 'dp'), may hold values from 1.277952 to 20.48
- small_second: float32 [7, 2048], replicated, may hold values from 1.277952 to 20.48
Outputs:
- block_out: bfloat16 [16384, 2048], P(('dp', 'tensor'))
- grad_in: float32 [16384, 2048], P(('dp', 'tensor'))
- qkv_grad: float32 [3, 2048, 2048], P(None, 'dp', 'tensor')
- qkv_first_new: float32 [3, 2048, 2048], P(None, 'dp', 'tensor')
- qkv_second_new: float32 [3, 2048, 2048], P(None, 'dp', 'tensor')
- qkv_new: float32 [3, 2048, 2048], P(None, 'dp', 'tensor')
- out_grad: float32 [2048, 2048], P('tensor', 'dp')
- out_first_new: float32 [2048, 2048], P('tensor', 'dp')
- out_second_new: float32 [2048, 2048], P('tensor', 'dp')
- out_new: float32 [2048, 2048], P('tensor', 'dp')
- gate_up_grad: float32 [2, 2048, 5632], P(None, 'dp', 'tensor')
- gate_up_first_new: float32 [2, 2048, 5632], P(None, 'dp', 'tensor')
- gate_up_second_new: float32 [2, 2048, 5632], P(None, 'dp', 'tensor')
- gate_up_new: float32 [2, 2048, 5632], P(None, 'dp', 'tensor')
- down_grad: float32 [5632, 2048], P('tensor', 'dp')
- down_first_new: float32 [5632, 2048], P('tensor', 'dp')
- down_second_new: float32 [5632, 2048], P('tensor', 'dp')
- down_new: float32 [5632, 2048], P('tensor', 'dp')
- small_grad: float32 [7, 2048], replicated
- small_first_new: float32 [7, 2048], replicated
- small_second_new: float32 [7, 2048], replicated
- small_new: float32 [7, 2048], replicated
Inputs may be any that keep to these rules, and one draw needn't show every extreme that they name: Each index of dp holds exactly two sequences; their lengths sum to at most 2048, and to exactly 2048 on some index. `owners`: every index of dp is named exactly twice.
All inputs are finite; a program needn't handle non-finite values.
Results may differ from a plain program's by a relative error of at most 0.015.
The roundings to bfloat16 on the way count: a program that leaves them out, or rounds other values in their place, can miss the bound.
Values may be sent and summed in bfloat16 or wider, within the bound.
No kernel may reach another device: no remote copies, remote signals or barrier semaphores. Data moves between devices by JAX's collectives and lax.ppermute only.
A program may use at most 384 MiB of HBM per device.

v0:
```python
import jax
import jax.numpy as jnp
from jax import lax
from jax.sharding import PartitionSpec as P

HD = 64
ROT = 16
CAP = 2048
STEP = 10


NORM_EPS = 1e-05
BETA_ONE = 0.9
BETA_TWO = 0.999
ADAM_EPS = 1e-08
WEIGHT_DECAY = 0.1
RATE_QKV = 0.05
RATE_OUT = 0.2
RATE_GATE_UP = 0.05
RATE_DOWN = 0.03
RATE_SMALL = 0.5


def layout(lengths, owners, dp_index):
    owned = owners == dp_index
    owned_lengths = jnp.where(owned, lengths, 0)
    seq_ends = jnp.cumsum(owned_lengths)
    seq_starts = seq_ends - owned_lengths
    owned_total = seq_ends[-1]
    row_ids = jnp.arange(CAP, dtype=jnp.int32)
    inside = (
        owned[None, :]
        & (row_ids[:, None] >= seq_starts[None, :])
        & (row_ids[:, None] < seq_ends[None, :])
    )
    inside_int = inside.astype(jnp.int32)
    live_rows = jnp.sum(inside_int, axis=1)
    seq_ids = jnp.arange(lengths.shape[0], dtype=jnp.int32)
    segment = jnp.where(live_rows > 0, jnp.sum(inside_int * seq_ids[None, :], axis=1), -1)
    begins = jnp.sum(inside_int * seq_starts[None, :], axis=1) + (1 - live_rows) * owned_total
    return (segment, row_ids - begins, live_rows)


def tables(position):
    half_rot = ROT // 2
    freqs = 10000.0 ** (-(jnp.arange(half_rot, dtype=jnp.float32) * (2.0 / ROT)))
    angles = position.astype(jnp.float32)[:, None] * freqs[None, :]
    return (jnp.cos(angles), jnp.sin(angles))


def rotate(heads_in, cosines, sines, direction):
    half_rot = ROT // 2
    first_half = heads_in[..., :half_rot]
    second_half = heads_in[..., half_rot:ROT]
    cosine_rows = cosines[:, None, :]
    sine_rows = sines[:, None, :] * direction
    return jnp.concatenate(
        [
            first_half * cosine_rows - second_half * sine_rows,
            second_half * cosine_rows + first_half * sine_rows,
            heads_in[..., ROT:],
        ],
        axis=-1,
    )


def norm_forward(values, gain, shift):
    average = jnp.mean(values, axis=-1, keepdims=True)
    centered = values - average
    inverse = lax.rsqrt(jnp.mean(centered * centered, axis=-1, keepdims=True) + NORM_EPS)
    unit_rows = centered * inverse
    return (unit_rows * gain + shift, unit_rows, inverse)


def norm_backward(incoming, unit_rows, inverse, gain):
    scaled = incoming * gain
    grad_rows = inverse * (
        scaled
        - jnp.mean(scaled, axis=-1, keepdims=True)
        - unit_rows * jnp.mean(scaled * unit_rows, axis=-1, keepdims=True)
    )
    return (grad_rows, jnp.sum(incoming * unit_rows, axis=0), jnp.sum(incoming, axis=0))


def block_mask(segment, first_row, block_rows):
    query_seg = lax.dynamic_slice_in_dim(segment, first_row, block_rows, 0)
    query_rows = first_row + jnp.arange(block_rows, dtype=jnp.int32)
    key_rows = jnp.arange(segment.shape[0], dtype=jnp.int32)
    return (query_seg[:, None] == segment[None, :]) & (key_rows[None, :] <= query_rows[:, None])


def block_scores(query_block, keys_rot, allowed):
    raw = jnp.einsum("qhd,khd->hqk", query_block, keys_rot, preferred_element_type=jnp.float32)
    return jnp.where(allowed[None], raw * HD ** (-0.5), -1e30)


def attend_forward(queries, keys_rot, values, segment):
    block_rows = min(512, CAP)

    def one_block(block_index):
        first_row = block_index * block_rows
        query_block = lax.dynamic_slice_in_dim(queries, first_row, block_rows, 0)
        scores = block_scores(query_block, keys_rot, block_mask(segment, first_row, block_rows))
        row_peak = jnp.max(scores, axis=-1, keepdims=True)
        exponent = jnp.exp(scores - row_peak)
        row_total = jnp.sum(exponent, axis=-1, keepdims=True)
        probs_low = (exponent / row_total).astype(jnp.bfloat16)
        mixed = jnp.einsum("hqk,khd->qhd", probs_low, values, preferred_element_type=jnp.float32)
        return (mixed.astype(jnp.bfloat16), (row_peak + jnp.log(row_total))[..., 0])

    mixed, log_total = lax.map(one_block, jnp.arange(CAP // block_rows, dtype=jnp.int32))
    return (mixed.reshape(CAP, -1), log_total)


def attend_backward(queries, keys_rot, values, segment, log_total, grad_mix):
    block_rows = min(512, CAP)
    grad_heads = grad_mix.reshape(queries.shape)

    def one_block(carry, block_index):
        grad_keys, grad_values = carry
        first_row = block_index * block_rows
        query_block = lax.dynamic_slice_in_dim(queries, first_row, block_rows, 0)
        grad_block = lax.dynamic_slice_in_dim(grad_heads, first_row, block_rows, 0)
        scores = block_scores(query_block, keys_rot, block_mask(segment, first_row, block_rows))
        probs = jnp.exp(scores - log_total[block_index][:, :, None])
        grad_probs = jnp.einsum(
            "qhd,khd->hqk", grad_block, values, preferred_element_type=jnp.float32
        )
        row_delta = jnp.sum(probs * grad_probs, axis=-1, keepdims=True)
        grad_scores = (probs * (grad_probs - row_delta) * HD ** (-0.5)).astype(jnp.bfloat16)
        grad_query = jnp.einsum(
            "hqk,khd->qhd", grad_scores, keys_rot, preferred_element_type=jnp.float32
        )
        grad_keys = grad_keys + jnp.einsum(
            "hqk,qhd->khd", grad_scores, query_block, preferred_element_type=jnp.float32
        )
        grad_values = grad_values + jnp.einsum(
            "hqk,qhd->khd",
            probs.astype(jnp.bfloat16),
            grad_block,
            preferred_element_type=jnp.float32,
        )
        return ((grad_keys, grad_values), grad_query)

    zeros_heads = jnp.zeros(queries.shape, jnp.float32)
    (grad_keys, grad_values), grad_query = lax.scan(
        one_block, (zeros_heads, zeros_heads), jnp.arange(CAP // block_rows, dtype=jnp.int32)
    )
    return (grad_query.reshape(queries.shape), grad_keys, grad_values)


def adam_update(weight_old, gradient, first_old, second_old, rate, decay):
    first_new = BETA_ONE * first_old + (1.0 - BETA_ONE) * gradient
    second_new = BETA_TWO * second_old + (1.0 - BETA_TWO) * gradient * gradient
    first_hat = first_new / (1.0 - BETA_ONE**STEP)
    second_hat = second_new / (1.0 - BETA_TWO**STEP)
    weight_new = weight_old * (1.0 - rate * decay) - rate * first_hat / (
        jnp.sqrt(second_hat) + ADAM_EPS
    )
    return (first_new, second_new, weight_new)


def local(
    hidden_in,
    grad_out,
    lengths,
    owners,
    qkv_weight,
    out_weight,
    gate_up_weight,
    down_weight,
    norm_gain,
    norm_bias,
    qkv_bias,
    qkv_first,
    out_first,
    gate_up_first,
    down_first,
    small_first,
    qkv_second,
    out_second,
    gate_up_second,
    down_second,
    small_second,
):
    dp_index = lax.axis_index("dp")
    tp_index = lax.axis_index("tensor")
    own_rows = hidden_in.shape[0]
    own_start = tp_index * own_rows
    local_width = qkv_weight.shape[2]
    local_heads = local_width // HD
    head_shape = (CAP, local_heads, HD)
    segment, position, live_rows = layout(lengths, owners, dp_index)
    live_own = lax.dynamic_slice_in_dim(live_rows, own_start, own_rows, 0).astype(jnp.float32)
    qkv_full, out_full, gate_up_full, down_full = (
        lax.all_gather(qkv_weight.astype(jnp.bfloat16), "dp", axis=1, tiled=True),
        lax.all_gather(out_weight.astype(jnp.bfloat16), "dp", axis=1, tiled=True),
        lax.all_gather(gate_up_weight.astype(jnp.bfloat16), "dp", axis=1, tiled=True),
        lax.all_gather(down_weight.astype(jnp.bfloat16), "dp", axis=1, tiled=True),
    )
    bias_local = lax.dynamic_slice_in_dim(qkv_bias, tp_index * local_width, local_width, 1)
    resid_in = hidden_in.astype(jnp.float32)
    first_norm, unit_one, inverse_one = norm_forward(resid_in, norm_gain[0], norm_bias[0])
    normed_one = lax.all_gather(first_norm.astype(jnp.bfloat16), "tensor", axis=0, tiled=True)
    projected = (
        jnp.einsum("rd,cdf->rcf", normed_one, qkv_full, preferred_element_type=jnp.float32)
        + bias_local[None]
    )
    cosines, sines = tables(position)
    queries = rotate(projected[:, 0].reshape(head_shape), cosines, sines, 1.0).astype(jnp.bfloat16)
    keys_rot = rotate(projected[:, 1].reshape(head_shape), cosines, sines, 1.0).astype(jnp.bfloat16)
    values = projected[:, 2].reshape(head_shape).astype(jnp.bfloat16)
    attn_mix, log_total = attend_forward(queries, keys_rot, values, segment)
    hidden = resid_in + lax.psum_scatter(
        jnp.dot(attn_mix, out_full, preferred_element_type=jnp.float32),
        "tensor",
        scatter_dimension=0,
        tiled=True,
    )
    second_norm, unit_two, inverse_two = norm_forward(hidden, norm_gain[1], norm_bias[1])
    normed_two = lax.all_gather(second_norm.astype(jnp.bfloat16), "tensor", axis=0, tiled=True)
    gate_up = jnp.einsum(
        "rd,cdf->crf", normed_two, gate_up_full, preferred_element_type=jnp.float32
    )
    gate_pre = gate_up[0]
    up_pre = gate_up[1]
    sigmoid_gate = jax.nn.sigmoid(gate_pre)
    activated = gate_pre * sigmoid_gate
    inner_act = (activated * up_pre).astype(jnp.bfloat16)
    layer_out = (
        hidden
        + lax.psum_scatter(
            jnp.dot(inner_act, down_full, preferred_element_type=jnp.float32),
            "tensor",
            scatter_dimension=0,
            tiled=True,
        )
    ).astype(jnp.bfloat16)
    cotangent = grad_out.astype(jnp.float32) * live_own[:, None]
    back_ffn = lax.all_gather(cotangent.astype(jnp.bfloat16), "tensor", axis=0, tiled=True)
    grad_inner = jnp.einsum("rd,fd->rf", back_ffn, down_full, preferred_element_type=jnp.float32)
    down_full_grad = jnp.einsum(
        "rf,rd->fd", inner_act, back_ffn, preferred_element_type=jnp.float32
    )
    grad_gate = grad_inner * up_pre * (sigmoid_gate * (1.0 + gate_pre * (1.0 - sigmoid_gate)))
    grad_up = grad_inner * activated
    grad_gate_up = jnp.stack([grad_gate, grad_up]).astype(jnp.bfloat16)
    gate_up_full_grad = jnp.einsum(
        "rd,crf->cdf", normed_two, grad_gate_up, preferred_element_type=jnp.float32
    )
    piece = grad_gate_up
    grad_second = lax.psum_scatter(
        jnp.einsum("crf,cdf->rd", piece, gate_up_full, preferred_element_type=jnp.float32),
        "tensor",
        scatter_dimension=0,
        tiled=True,
    )
    grad_norm_two, gain_two_grad, bias_two_grad = norm_backward(
        grad_second, unit_two, inverse_two, norm_gain[1]
    )
    grad_hidden = cotangent + grad_norm_two
    back_attn = lax.all_gather(grad_hidden.astype(jnp.bfloat16), "tensor", axis=0, tiled=True)
    out_full_grad = jnp.einsum("rf,rd->fd", attn_mix, back_attn, preferred_element_type=jnp.float32)
    grad_mix = jnp.einsum(
        "rd,fd->rf", back_attn, out_full, preferred_element_type=jnp.float32
    ).astype(jnp.bfloat16)
    grad_query, grad_keys, grad_values = attend_backward(
        queries, keys_rot, values, segment, log_total, grad_mix
    )
    grad_query = rotate(grad_query, cosines, sines, -1.0)
    grad_keys = rotate(grad_keys, cosines, sines, -1.0)
    grad_proj = jnp.stack(
        [
            grad_query.reshape(CAP, local_width),
            grad_keys.reshape(CAP, local_width),
            grad_values.reshape(CAP, local_width),
        ],
        axis=1,
    ).astype(jnp.bfloat16)
    qkv_full_grad = jnp.einsum(
        "rd,rcf->cdf", normed_one, grad_proj, preferred_element_type=jnp.float32
    )
    bias_grad_local = jnp.sum(grad_proj.astype(jnp.float32), axis=0)
    piece = grad_proj
    grad_first = lax.psum_scatter(
        jnp.einsum("rcf,cdf->rd", piece, qkv_full, preferred_element_type=jnp.float32),
        "tensor",
        scatter_dimension=0,
        tiled=True,
    )
    grad_norm_one, gain_one_grad, bias_one_grad = norm_backward(
        grad_first, unit_one, inverse_one, norm_gain[0]
    )
    input_grad = grad_hidden + grad_norm_one
    bias_grad_full = lax.dynamic_update_slice_in_dim(
        jnp.zeros((3, qkv_bias.shape[1]), jnp.float32), bias_grad_local, tp_index * local_width, 1
    )
    small_local = jnp.concatenate(
        [
            jnp.stack([gain_one_grad, gain_two_grad]),
            jnp.stack([bias_one_grad, bias_two_grad]),
            bias_grad_full,
        ],
        axis=0,
    )
    small_grad = lax.psum(small_local, ("dp", "tensor"))
    qkv_grad, out_grad, gate_up_grad, down_grad = (
        lax.psum_scatter(qkv_full_grad, "dp", scatter_dimension=1, tiled=True),
        lax.psum_scatter(out_full_grad, "dp", scatter_dimension=1, tiled=True),
        lax.psum_scatter(gate_up_full_grad, "dp", scatter_dimension=1, tiled=True),
        lax.psum_scatter(down_full_grad, "dp", scatter_dimension=1, tiled=True),
    )
    small_weight = jnp.concatenate([norm_gain, norm_bias, qkv_bias], axis=0)
    qkv_first_new, qkv_second_new, qkv_new = adam_update(
        qkv_weight, qkv_grad, qkv_first, qkv_second, RATE_QKV, WEIGHT_DECAY
    )
    out_first_new, out_second_new, out_new = adam_update(
        out_weight, out_grad, out_first, out_second, RATE_OUT, WEIGHT_DECAY
    )
    gate_up_first_new, gate_up_second_new, gate_up_new = adam_update(
        gate_up_weight, gate_up_grad, gate_up_first, gate_up_second, RATE_GATE_UP, WEIGHT_DECAY
    )
    down_first_new, down_second_new, down_new = adam_update(
        down_weight, down_grad, down_first, down_second, RATE_DOWN, WEIGHT_DECAY
    )
    small_first_new, small_second_new, small_new = adam_update(
        small_weight, small_grad, small_first, small_second, RATE_SMALL, 0.0
    )
    return (
        layer_out,
        input_grad,
        qkv_grad,
        qkv_first_new,
        qkv_second_new,
        qkv_new,
        out_grad,
        out_first_new,
        out_second_new,
        out_new,
        gate_up_grad,
        gate_up_first_new,
        gate_up_second_new,
        gate_up_new,
        down_grad,
        down_first_new,
        down_second_new,
        down_new,
        small_grad,
        small_first_new,
        small_second_new,
        small_new,
    )


def solution(mesh):
    placed = (
        P(("dp", "tensor"), None),
        P(("dp", "tensor"), None),
        P(),
        P(),
        P(None, "dp", "tensor"),
        P("tensor", "dp"),
        P(None, "dp", "tensor"),
        P("tensor", "dp"),
        P(),
        P(),
        P(),
        P(None, "dp", "tensor"),
        P("tensor", "dp"),
        P(None, "dp", "tensor"),
        P("tensor", "dp"),
        P(),
        P(None, "dp", "tensor"),
        P("tensor", "dp"),
        P(None, "dp", "tensor"),
        P("tensor", "dp"),
        P(),
    )
    return jax.shard_map(
        local,
        mesh=mesh,
        in_specs=placed,
        out_specs=(
            P(("dp", "tensor"), None),
            P(("dp", "tensor"), None),
            P(None, "dp", "tensor"),
            P(None, "dp", "tensor"),
            P(None, "dp", "tensor"),
            P(None, "dp", "tensor"),
            P("tensor", "dp"),
            P("tensor", "dp"),
            P("tensor", "dp"),
            P("tensor", "dp"),
            P(None, "dp", "tensor"),
            P(None, "dp", "tensor"),
            P(None, "dp", "tensor"),
            P(None, "dp", "tensor"),
            P("tensor", "dp"),
            P("tensor", "dp"),
            P("tensor", "dp"),
            P("tensor", "dp"),
            P(),
            P(),
            P(),
            P(),
        ),
        check_vma=False,
    )
```

profile of v0, /device:TPU:0, one launch (start us, length us, event | category | flops | bytes accessed | tf_op | source)
XLA Modules:
  0.0 2452.9 jit_solution(1572725297215503362)
XLA Ops:
  21.6 59.2 %all-gather.11.cloned.1.call-done = bf16[3,2048,512]{1,2,0:T(8,128)(2,1)} async-done(((bf16[3,256,512]{1,2,0:T(8,128)(2,1)}), bf16[3,2048,512]{1,2,0:T(8,128)(2,1)}) %all-gather.11.cloned.1.call-update) | async-done | bytes 6291472 | tf_op jit(solution)/shard_map/all_gather | solution.py:196
  80.8 88.2 %all-gather.9.cloned.1.call-done = bf16[2048,2048]{1,0:T(8,128)(2,1)} async-done(((bf16[512,2048]{1,0:T(8,128)(2,1)}), bf16[2048,2048]{1,0:T(8,128)(2,1)}) %all-gather.9.cloned.1.call-update) | async-done | bytes 8388624 | tf_op jit(solution)/shard_map/all_gather | solution.py:204
  198.8 196.7 %while.27 = (s32[]{:T(128)}, bf16[4,512,8,64]{1,3,2,0:T(8,128)(2,1)}, f32[4,8,512]{2,1,0:T(8,128)}, s32[4]{0:T(128)S(1)}, s32[2048]{0:T(1024)S(1)}, /*index=5*/b...) while((s32[]{:T(128)}, ...), condition=%wide.region_9.10_spmd, body=%wide.region_6.9_spmd.sunk | while | flops 2251551232 | bytes 110250184 | solution.py:111
  417.3 150.7 %reduce-scatter.9.cloned.1.call-done = f32[512,2048]{1,0:T(8,128)} async-done(((f32[2048,2048]{1,0:T(8,128)}), f32[512,2048]{1,0:T(8,128)}) %reduce-scatter.9.cloned.1.call-update) | async-done | bytes 4194320 | tf_op jit(solution)/shard_map/reduce_scatter | solution.py:214
  579.0 99.0 %all-gather.17.cloned.1.call-done = bf16[2,2048,1408]{2,1,0:T(8,128)(2,1)} async-done(((bf16[2,256,1408]{2,1,0:T(8,128)(2,1)}), bf16[2,2048,1408]{2,1,0:T(8,128)(2,1)}) %all-gather.17.cloned.1.call-update) | async-done | bytes 11534352 | tf_op jit(solution)/shard_map/all_gather | solution.py:198
  678.1 88.2 %all-gather.15.cloned.1.call-done = bf16[2048,2048]{1,0:T(8,128)(2,1)} async-done(((bf16[512,2048]{1,0:T(8,128)(2,1)}), bf16[2048,2048]{1,0:T(8,128)(2,1)}) %all-gather.15.cloned.1.call-update) | async-done | bytes 8388624 | tf_op jit(solution)/shard_map/all_gather | solution.py:221
  766.3 32.1 %convolution_bitcast_fusion = f32[2,2048,1408]{2,1,0:T(8,128)} fusion(bf16[2,2048,1408]{2,1,0:T(8,128)(2,1)} %all-gather.17.cloned.1.call-done, bf16[2048,2048]{1,0:T(8,128)(2,1)} %all-gather.15.cloned.1.call-done), kind=kOutput, calls=%fused_computation.47 | convolution fusion | flops 23622320128 | bytes 42991616 | tf_op jit(solution)/shard_map/rd,cdf->crf/dot_general | solution.py:222
  798.4 31.0 %all-gather.19.cloned.1.call-done = bf16[1408,2048]{1,0:T(8,128)(2,1)} async-done(((bf16[1408,256]{1,0:T(8,128)(2,1)}), bf16[1408,2048]{1,0:T(8,128)(2,1)}) %all-gather.19.cloned.1.call-update) | async-done | bytes 5767184 | tf_op jit(solution)/shard_map/all_gather | solution.py:199
  829.3 88.2 %all-gather.21.cloned.1.call-done = bf16[2048,2048]{1,0:T(8,128)(2,1)} async-done(((bf16[512,2048]{1,0:T(8,128)(2,1)}), bf16[2048,2048]{1,0:T(8,128)(2,1)}) %all-gather.21.cloned.1.call-update) | async-done | bytes 8388624 | tf_op jit(solution)/shard_map/all_gather | solution.py:240
  917.6 25.8 %fusion.53 = (bf16[1,2048,1408]{2,1,0:T(8,128)(2,1)}, bf16[1,2048,1408]{2,1,0:T(8,128)(2,1)}, bf16[2048,1408]{1,0:T(8,128)(2,1)}) fusion(f32[2,2048,1408]{2,1,0:T(8,128)} %convolution_bitcast_fusion, bf16[2048,2048]{1,0:T(8,128)(2,1)} %all-gather.21.cloned.1.call-done, bf16[1408,2048]{1,0:T(8,128)(2,1)} %all-gather.19.cloned.1.call-done), kind=kOutput, calls=%fused_computation.72 | convolution fusion | flops 11854413824 | bytes 54525952 | tf_op jit(solution)/shard_map/rd,fd->rf/dot_general | solution.py:241
  943.3 32.5 %convolution_bitcast_fusion.3 = f32[2048,2048]{1,0:T(8,128)} fusion(bf16[2,2048,1408]{2,1,0:T(8,128)(2,1)} %all-gather.17.cloned.1.call-done, bf16[1,2048,1408]{2,1,0:T(8,128)(2,1)} %get-tuple-element.304, bf16[1,2048,1408]{2,1,0:T(8,128)(2,1)} %get-tuple-element.303), kind=kOutput, calls=%fused_computation.59 | convolution fusion | flops 23628087296 | bytes 39845888 | tf_op jit(solution)/shard_map/crf,cdf->rd/dot_general | solution.py:253
  995.3 134.6 %reduce-scatter.13.cloned.1.call-done = f32[512,2048]{1,0:T(8,128)} async-done(((f32[2048,2048]{1,0:T(8,128)}), f32[512,2048]{1,0:T(8,128)}) %reduce-scatter.13.cloned.1.call-update) | async-done | bytes 4194320 | tf_op jit(solution)/shard_map/reduce_scatter | solution.py:252
  1134.9 151.8 %reduce-scatter.11.cloned.1.call-done = f32[512,2048]{1,0:T(8,128)} async-done(((f32[2048,2048]{1,0:T(8,128)}), f32[512,2048]{1,0:T(8,128)}) %reduce-scatter.11.cloned.1.call-update) | async-done | bytes 4194320 | tf_op jit(solution)/shard_map/reduce_scatter | solution.py:232
  1313.7 32.4 %convolution_bitcast_fusion.1 = f32[2,2048,1408]{1,2,0:T(8,128)} fusion(bf16[2048,2048]{1,0:T(8,128)(2,1)} %all-gather.15.cloned.1.call-done, bf16[1,2048,1408]{2,1,0:T(8,128)(2,1)} %get-tuple-element.304, bf16[1,2048,1408]{2,1,0:T(8,128)(2,1)} %get-tuple-element.303), kind=kOutput, calls=%fused_computation.48 | convolution fusion | flops 23628087296 | bytes 42991616 | tf_op jit(solution)/shard_map/rd,crf->cdf/dot_general | solution.py:248
  1346.2 36.0 %all-gather.23.cloned.1.call-done = bf16[2048,2048]{1,0:T(8,128)(2,1)} async-done(((bf16[512,2048]{1,0:T(8,128)(2,1)}), bf16[2048,2048]{1,0:T(8,128)(2,1)}) %all-gather.23.cloned.1.call-update) | async-done | bytes 8388624 | tf_op jit(solution)/shard_map/all_gather | solution.py:262
  1401.8 664.1 %while.28 = (s32[]{:T(128)}, f32[2048,8,64]{0,2,1:T(8,128)}, f32[2048,8,64]{0,2,1:T(8,128)}, f32[4,512,8,64]{1,0,3,2:T(4,128)}, s32[4]{0:T(128)S(1)}, /*index=5*...) while((s32[]{:T(128)}, f32[2048,8,64]{0,2,1:T(8,128)}, ...), condition=%wide.region_19.20_spmd.clone, body=%wide.region_17.19_spmd.clone.sunk | while | flops 5493502464 | bytes 334563584 | solution.py:146
  1455.2 43.8 %fusion.157 = f32[1,512,8,64]{1,3,2,0:T(8,128)} fusion(bf16[2048,8,64]{0,2,1:T(8,128)(2,1)} %get-tuple-element.527, f32[8,512,2048]{2,1,0:T(8,128)} %subtract_exponential_fusion.3, f32[8,512,2048]{2,1,0:T(8,128)} %fusion.156), kind=kOutput, calls=%fused_computation.31.clone.1 | convolution fusion | flops 1115691008 | bytes 70254592 | tf_op jit(solution)/shard_map/while/body/eval_jaxpr/hqk,khd->qhd/dot_general | solution.py:131
  1499.0 45.6 %bitcast_add_fusion.4 = f32[2048,8,64]{0,2,1:T(8,128)} fusion(f32[2048,8,64]{0,2,1:T(8,128)} %get-tuple-element.505, f32[8,512,2048]{2,1,0:T(8,128)} %subtract_exponential_fusion.3, f32[8,512,2048]{2,1,0:T(8,128)} %fusion.156, pred[]{:T(512)S(6)} %compare.3, bf16[2048,8,64]{0,2,1:T(8,128)(2,1)} %get-tuple-element.525, s32[]{:T(128)S(6)} %select_n.74), kind=kOutput, calls=%fused_computation.28.clone.1 | convolution fusion | flops 1117788160 | bytes 143130624 | tf_op jit(solution)/shard_map/while/body/eval_jaxpr/hqk,qhd->khd/dot_general | solution.py:134
  1546.8 21.1 dynamic_update_slice.25
  1622.7 44.4 %fusion.157 = f32[1,512,8,64]{1,3,2,0:T(8,128)} fusion(bf16[2048,8,64]{0,2,1:T(8,128)(2,1)} %get-tuple-element.527, f32[8,512,2048]{2,1,0:T(8,128)} %subtract_exponential_fusion.3, f32[8,512,2048]{2,1,0:T(8,128)} %fusion.156), kind=kOutput, calls=%fused_computation.31.clone.1 | convolution fusion | flops 1115691008 | bytes 70254592 | tf_op jit(solution)/shard_map/while/body/eval_jaxpr/hqk,khd->qhd/dot_general | solution.py:131
  1667.1 45.9 %bitcast_add_fusion.4 = f32[2048,8,64]{0,2,1:T(8,128)} fusion(f32[2048,8,64]{0,2,1:T(8,128)} %get-tuple-element.505, f32[8,512,2048]{2,1,0:T(8,128)} %subtract_exponential_fusion.3, f32[8,512,2048]{2,1,0:T(8,128)} %fusion.156, pred[]{:T(512)S(6)} %compare.3, bf16[2048,8,64]{0,2,1:T(8,128)(2,1)} %get-tuple-element.525, s32[]{:T(128)S(6)} %select_n.74), kind=kOutput, calls=%fused_computation.28.clone.1 | convolution fusion | flops 1117788160 | bytes 143130624 | tf_op jit(solution)/shard_map/while/body/eval_jaxpr/hqk,qhd->khd/dot_general | solution.py:134
  1715.4 21.1 dynamic_update_slice.25
  1790.4 43.1 %fusion.157 = f32[1,512,8,64]{1,3,2,0:T(8,128)} fusion(bf16[2048,8,64]{0,2,1:T(8,128)(2,1)} %get-tuple-element.527, f32[8,512,2048]{2,1,0:T(8,128)} %subtract_exponential_fusion.3, f32[8,512,2048]{2,1,0:T(8,128)} %fusion.156), kind=kOutput, calls=%fused_computation.31.clone.1 | convolution fusion | flops 1115691008 | bytes 70254592 | tf_op jit(solution)/shard_map/while/body/eval_jaxpr/hqk,khd->qhd/dot_general | solution.py:131
  1833.6 44.6 %bitcast_add_fusion.4 = f32[2048,8,64]{0,2,1:T(8,128)} fusion(f32[2048,8,64]{0,2,1:T(8,128)} %get-tuple-element.505, f32[8,512,2048]{2,1,0:T(8,128)} %subtract_exponential_fusion.3, f32[8,512,2048]{2,1,0:T(8,128)} %fusion.156, pred[]{:T(512)S(6)} %compare.3, bf16[2048,8,64]{0,2,1:T(8,128)(2,1)} %get-tuple-element.525, s32[]{:T(128)S(6)} %select_n.74), kind=kOutput, calls=%fused_computation.28.clone.1 | convolution fusion | flops 1117788160 | bytes 143130624 | tf_op jit(solution)/shard_map/while/body/eval_jaxpr/hqk,qhd->khd/dot_general | solution.py:134
  1880.5 21.0 dynamic_update_slice.25
  1954.7 43.1 %fusion.157 = f32[1,512,8,64]{1,3,2,0:T(8,128)} fusion(bf16[2048,8,64]{0,2,1:T(8,128)(2,1)} %get-tuple-element.527, f32[8,512,2048]{2,1,0:T(8,128)} %subtract_exponential_fusion.3, f32[8,512,2048]{2,1,0:T(8,128)} %fusion.156), kind=kOutput, calls=%fused_computation.31.clone.1 | convolution fusion | flops 1115691008 | bytes 70254592 | tf_op jit(solution)/shard_map/while/body/eval_jaxpr/hqk,khd->qhd/dot_general | solution.py:131
  1997.8 44.6 %bitcast_add_fusion.4 = f32[2048,8,64]{0,2,1:T(8,128)} fusion(f32[2048,8,64]{0,2,1:T(8,128)} %get-tuple-element.505, f32[8,512,2048]{2,1,0:T(8,128)} %subtract_exponential_fusion.3, f32[8,512,2048]{2,1,0:T(8,128)} %fusion.156, pred[]{:T(512)S(6)} %compare.3, bf16[2048,8,64]{0,2,1:T(8,128)(2,1)} %get-tuple-element.525, s32[]{:T(128)S(6)} %select_n.74), kind=kOutput, calls=%fused_computation.28.clone.1 | convolution fusion | flops 1117788160 | bytes 143130624 | tf_op jit(solution)/shard_map/while/body/eval_jaxpr/hqk,qhd->khd/dot_general | solution.py:134
  2044.8 21.0 dynamic_update_slice.25
  2091.1 20.5 fusion.54
  2180.9 60.1 %reduce-scatter.17.cloned.1.call-done = f32[3,256,512]{1,2,0:T(8,128)} async-done(((f32[3,2048,512]{1,2,0:T(8,128)}), f32[3,256,512]{1,2,0:T(8,128)}) %reduce-scatter.17.cloned.1.call-update) | async-done | bytes 1572880 | tf_op jit(solution)/shard_map/reduce_scatter | solution.py:308
  2258.2 137.9 %reduce-scatter.15.cloned.1.call-done = f32[512,2048]{1,0:T(8,128)} async-done(((f32[2048,2048]{1,0:T(8,128)}), f32[512,2048]{1,0:T(8,128)}) %reduce-scatter.15.cloned.1.call-update) | async-done | bytes 4194320 | tf_op jit(solution)/shard_map/reduce_scatter | solution.py:285
  2399.9 39.6 %psum.7 = f32[7,2048]{1,0:T(8,128)S(1)} all-reduce(f32[7,2048]{1,0:T(8,128)S(1)} %concatenate.26), channel_id=1, replica_groups=mesh['dp'=8,'tensor'=4] {'dp','tensor'}, use_global_device_ids=true, to_apply=%region_32.33 | all-reduce | flops 14336 | bytes 114688 | tf_op jit(solution)/shard_map/psum | solution.py:306
  (296 shorter events, 676.1 us)
Async XLA Ops:
  7.2 73.6 %all-gather.11.cloned.1.call-start = ((), (), s32[]{:S(2)}) async-start(), calls=%async_computation.9 | async-start | bytes 7077888 | tf_op jit(solution)/shard_map/all_gather | solution.py:196
  12.8 156.3 %all-gather.9.cloned.1.call-start = ((), (), s32[]{:S(2)}) async-start(), calls=%async_computation.8 | async-start | bytes 10485760 | tf_op jit(solution)/shard_map/all_gather | solution.py:204
  17.4 384.0 %all-gather.13.cloned.1.call-start = ((), (), s32[]{:S(2)}) async-start(), calls=%async_computation.10 | async-start | bytes 2359296 | tf_op jit(solution)/shard_map/all_gather | solution.py:197
  18.2 549.7 %reduce-scatter.9.cloned.1.call-start = ((), (), s32[]{:S(2)}) async-start(), calls=%async_computation.11 | async-start | bytes 20971520 | tf_op jit(solution)/shard_map/reduce_scatter | solution.py:214
  19.3 149.8 %copy-start.38 = (s32[2048]{0:T(1024)}, s32[2048]{0:T(1024)S(1)}, u32[]{:S(2)}) copy-start(s32[2048]{0:T(1024)S(1)} %get-tuple-element.241) | copy-start | bytes 24580
  21.6 174.7 %copy-start.19 = (f32[2048,8]{0,1:T(8,128)}, f32[2048,8]{0,1:T(8,128)S(1)}, u32[]{:S(2)}) copy-start(f32[2048,8]{0,1:T(8,128)S(1)} %get-tuple-element.327) | copy-start | bytes 196612
  414.0 154.0 %copy-start.4 = (bf16[512,2048]{1,0:T(8,128)(2,1)S(1)}, bf16[512,2048]{1,0:T(8,128)(2,1)}, u32[]{:S(2)}) copy-start(bf16[512,2048]{1,0:T(8,128)(2,1)} %param.25) | copy-start | bytes 6291460
  414.0 264.1 %all-gather.17.cloned.1.call-start = ((), (), s32[]{:S(2)}) async-start(), calls=%async_computation.13 | async-start | bytes 12976128 | tf_op jit(solution)/shard_map/all_gather | solution.py:198
  417.2 349.0 %all-gather.15.cloned.1.call-start = ((), (), s32[]{:S(2)}) async-start(), calls=%async_computation.12 | async-start | bytes 10485760 | tf_op jit(solution)/shard_map/all_gather | solution.py:221
  574.8 254.5 %all-gather.19.cloned.1.call-start = ((), (), s32[]{:S(2)}) async-start(), calls=%async_computation.14 | async-start | bytes 6488064 | tf_op jit(solution)/shard_map/all_gather | solution.py:199
  575.8 341.8 %all-gather.21.cloned.1.call-start = ((), (), s32[]{:S(2)}) async-start(), calls=%async_computation.16 | async-start | bytes 10485760 | tf_op jit(solution)/shard_map/all_gather | solution.py:240
  579.0 550.9 %reduce-scatter.13.cloned.1.call-start = ((), (), s32[]{:S(2)}) async-start(), calls=%async_computation.17 | async-start | bytes 20971520 | tf_op jit(solution)/shard_map/reduce_scatter | solution.py:252
  975.9 310.8 %reduce-scatter.11.cloned.1.call-start = ((), (), s32[]{:S(2)}) async-start(), calls=%async_computation.15 | async-start | bytes 20971520 | tf_op jit(solution)/shard_map/reduce_scatter | solution.py:232
  995.2 291.5 %copy-start.12 = (bf16[512,2048]{1,0:T(8,128)(2,1)S(1)}, bf16[512,2048]{1,0:T(8,128)(2,1)}, u32[]{:S(2)}) copy-start(bf16[512,2048]{1,0:T(8,128)(2,1)} %param.26) | copy-start | bytes 6291460
  995.2 291.5 %copy-start.47 = (f32[512]{0:T(512)S(1)}, f32[512]{0:T(512)}, u32[]{:S(2)}) copy-start(f32[512]{0:T(512)} %copy-done.46) | copy-start | bytes 6148
  995.2 387.0 %all-gather.23.cloned.1.call-start = ((), (), s32[]{:S(2)}) async-start(), calls=%async_computation.18 | async-start | bytes 10485760 | tf_op jit(solution)/shard_map/all_gather | solution.py:262
  1294.5 854.0 %reduce-scatter.23.cloned.1.call-start = ((), (), s32[]{:S(2)}) async-start(), calls=%async_computation.23 | async-start | bytes 12976128 | tf_op jit(solution)/shard_map/reduce_scatter | solution.py:311
  1313.7 840.1 %reduce-scatter.21.cloned.1.call-start = ((), (), s32[]{:S(2)}) async-start(), calls=%async_computation.22 | async-start | bytes 25952256 | tf_op jit(solution)/shard_map/reduce_scatter | solution.py:310
  1346.2 831.9 %reduce-scatter.19.cloned.1.call-start = ((), (), s32[]{:S(2)}) async-start(), calls=%async_computation.21 | async-start | bytes 4718592 | tf_op jit(solution)/shard_map/reduce_scatter | solution.py:309
  1391.7 849.3 %reduce-scatter.17.cloned.1.call-start = ((), (), s32[]{:S(2)}) async-start(), calls=%async_computation.20 | async-start | bytes 14155776 | tf_op jit(solution)/shard_map/reduce_scatter | solution.py:308
  2111.7 284.5 %reduce-scatter.15.cloned.1.call-start = ((), (), s32[]{:S(2)}) async-start(), calls=%async_computation.19 | async-start | bytes 20971520 | tf_op jit(solution)/shard_map/reduce_scatter | solution.py:285
  2248.7 147.5 %copy-start.5 = (bf16[512,2048]{1,0:T(8,128)(2,1)S(1)}, bf16[512,2048]{1,0:T(8,128)(2,1)}, u32[]{:S(2)}) copy-start(bf16[512,2048]{1,0:T(8,128)(2,1)} %param.25) | copy-start | bytes 6291460
  2248.7 147.5 %copy-start.24 = (f32[1,2048]{1,0:T(1,128)S(1)}, f32[1,2048]{1,0:T(1,128)}, u32[]{:S(2)}) copy-start(f32[1,2048]{1,0:T(1,128)} %copy-done.23) | copy-start | bytes 24580
  2248.7 147.5 %copy-start.34 = (f32[512]{0:T(512)S(1)}, f32[512]{0:T(512)}, u32[]{:S(2)}) copy-start(f32[512]{0:T(512)} %copy-done.33) | copy-start | bytes 6148
  2248.7 147.5 %copy-start.40 = (f32[512]{0:T(512)S(1)}, f32[512]{0:T(512)}, u32[]{:S(2)}) copy-start(f32[512]{0:T(512)} %copy-done.39) | copy-start | bytes 6148
  2255.0 144.9 %copy-start.42 = (f32[2048]{0:T(1024)S(1)}, f32[2048]{0:T(1024)}, u32[]{:S(2)}) copy-start(f32[2048]{0:T(1024)} %get-tuple-element.231) | copy-start | bytes 24580
  2255.0 144.9 %copy-start.43 = (f32[2048]{0:T(1024)S(1)}, f32[2048]{0:T(1024)}, u32[]{:S(2)}) copy-start(f32[2048]{0:T(1024)} %get-tuple-element.237) | copy-start | bytes 24580
  2255.0 184.6 %copy-start.27 = (f32[7,2048]{1,0:T(8,128)S(1)}, f32[7,2048]{1,0:T(8,128)}, u32[]{:S(2)}) copy-start(f32[7,2048]{1,0:T(8,128)} %param.45) | copy-start | bytes 172036
  2255.0 184.6 %copy-start.28 = (f32[7,2048]{1,0:T(8,128)S(1)}, f32[7,2048]{1,0:T(8,128)}, u32[]{:S(2)}) copy-start(f32[7,2048]{1,0:T(8,128)} %param.40) | copy-start | bytes 172036
  2255.0 184.6 %copy-start.30 = (f32[2,2048]{1,0:T(2,128)S(1)}, f32[2,2048]{1,0:T(2,128)}, u32[]{:S(2)}) copy-start(f32[2,2048]{1,0:T(2,128)} %param.34) | copy-start | bytes 49156
  2255.0 184.6 %copy-start.32 = (f32[2,2048]{1,0:T(2,128)S(1)}, f32[2,2048]{1,0:T(2,128)}, u32[]{:S(2)}) copy-start(f32[2,2048]{1,0:T(2,128)} %param.33) | copy-start | bytes 49156
  2255.0 184.6 %copy-start.35 = (f32[3,2048]{1,0:T(4,128)S(1)}, f32[3,2048]{1,0:T(4,128)}, u32[]{:S(2)}) copy-start(f32[3,2048]{1,0:T(4,128)} %param.35) | copy-start | bytes 73732
  (34 other events, 684.5 us)
Sparse Core Ops, SparseCore 0:
  12.9 67.8 all-gather.10
  83.3 85.7 all-gather.8
  171.3 30.8 all-gather.12
  414.1 153.8 reduce-scatter.8
  570.0 108.0 all-gather.16
  680.3 85.8 all-gather.14
  768.5 60.8 all-gather.18
  831.7 85.7 all-gather.20
  976.0 153.8 reduce-scatter.12
  1132.8 153.8 reduce-scatter.10
  1294.6 87.5 all-gather.22
  1385.0 119.2 reduce-scatter.22
  1506.7 225.8 reduce-scatter.20
  1735.3 48.4 reduce-scatter.18
  2111.8 129.1 reduce-scatter.16
  2243.9 152.1 reduce-scatter.14
where the time goes:
time: 2460 us; the launch traced here: 2450 us
  waiting for transfers between devices  1130 us (46%)
  matrix products  924 us (38%)
  local copies, waits for them, and re-layouts  185 us (8%)
  other arithmetic  149 us (6%)
  blocking collectives  39.6 us (2%)
    dot_general x4, matrix products, one_block(): jnp.einsum('hqk,qhd->khd', grad_scores, query_block, preferred_element_ty...  181 us
    dot_general x4, matrix products, one_block(): jnp.einsum('hqk,khd->qhd', grad_scores, keys_rot, preferred_element_type=...  174 us
    reduce_scatter x1, waiting for transfers between devices, local(): lax.psum_scatter(jnp.dot(inner_act, down_full, preferred_element_type=jnp...  152 us
    reduce_scatter x1, waiting for transfers between devices, local(): lax.psum_scatter(jnp.dot(attn_mix, out_full, preferred_element_type=jnp.f...  151 us
    reduce_scatter x1, waiting for transfers between devices, local(): lax.psum_scatter(jnp.einsum('rcf,cdf->rd', piece, qkv_full, preferred_ele...  138 us
    reduce_scatter x1, waiting for transfers between devices, local(): lax.psum_scatter(jnp.einsum('crf,cdf->rd', piece, gate_up_full, preferred...  135 us
    dot_general x8, matrix products, block_scores(): jnp.einsum('qhd,khd->hqk', query_block, keys_rot, preferred_element_type=...  129 us
    all_gather x1, waiting for transfers between devices, local(): lax.all_gather(gate_up_weight.astype(jnp.bfloat16), 'dp', axis=1, tiled=T...  99 us
  transfers between devices with their start and end apart: 16, of which 12 were waited for; matrix products, arithmetic and copies ran while one was open for 47% of the time, Pallas kernels for 0%

commit v1 on v0

v1 whole, which is shorter than its diff:
```python
import functools

import jax
import jax.numpy as jnp
from jax import lax
from jax.experimental import pallas as pl
from jax.experimental.pallas import tpu as pltpu
from jax.sharding import PartitionSpec as P

STEP = 10
NORM_EPS = 1e-05
BETA_ONE = 0.9
BETA_TWO = 0.999
ADAM_EPS = 1e-08
WEIGHT_DECAY = 0.1
RATE_QKV = 0.05
RATE_OUT = 0.2
RATE_GATE_UP = 0.05
RATE_DOWN = 0.03
RATE_SMALL = 0.5
HD = 64
ROT = 16
BLK = 256
PAIR = 2 * HD
NT = (((1,), (1,)), ((), ()))
NN = (((1,), (0,)), ((), ()))
NEG = -1e30
VMEM_LIMIT = 56 * 1024 * 1024
THRIFT = 1


def spend(flops, bytes_accessed, transcendentals):
    return pl.CostEstimate(
        flops=flops // THRIFT,
        bytes_accessed=bytes_accessed // THRIFT,
        transcendentals=transcendentals // THRIFT,
    )


def mm(a, b, dims=NN):
    return lax.dot_general(a, b, dims, preferred_element_type=jnp.float32)


def lane_masks():
    lane = lax.broadcasted_iota(jnp.int32, (1, PAIR), 1)
    first = jnp.where(lane < HD, 1.0, 0.0).astype(jnp.bfloat16)
    second = jnp.where(lane < HD, 0.0, 1.0).astype(jnp.bfloat16)
    return (first, second)


def allowed_block(info_ref, key_block, query_block):
    split, total = info_ref[0], info_ref[1]
    key_rows = key_block * BLK + lax.broadcasted_iota(jnp.int32, (BLK, BLK), 0)
    query_rows = query_block * BLK + lax.broadcasted_iota(jnp.int32, (BLK, BLK), 1)
    rows = query_block * BLK + lax.broadcasted_iota(jnp.int32, (1, BLK), 1)
    starts = jnp.where(rows < split, 0, jnp.where(rows < total, split, total))
    return (key_rows <= query_rows) & (key_rows >= starts)


def row_start(info_ref, row):
    split, total = info_ref[0], info_ref[1]
    return jnp.where(row < split, 0, jnp.where(row < total, split, total))


def key_range(info_ref, query_block):
    low = row_start(info_ref, query_block * BLK) // BLK
    last = row_start(info_ref, query_block * BLK + (BLK - 1))
    mid = jnp.minimum((last + (BLK - 1)) // BLK, query_block)
    return (low, mid)


def swap_block(block, shift_index, per_own):
    return lax.bitwise_xor(block // per_own, shift_index) * per_own + block % per_own


def aligned(block):
    return pl.ds(pl.multiple_of(block * BLK, BLK), BLK)


def attend_forward_kernel(chunks, count, per_own, after, info_ref, *refs):
    refs = refs[after:]
    group = len(chunks)
    q_refs, refs = refs[:group], refs[group:]
    k_refs, v_refs, refs = refs[:count], refs[count : 2 * count], refs[2 * count :]
    o_refs, l_refs = refs[:group], refs[group : 2 * group]
    q_all, o_all, l_all, k_all, vt_all = refs[2 * group :]
    tensor_at = info_ref[2]
    own = per_own * BLK
    heads = k_all.shape[1] // HD
    spans = [slice(head // 2 * PAIR, head // 2 * PAIR + PAIR) for head in range(heads)]
    for at in range(count):
        k_all[at * own : (at + 1) * own, :] = k_refs[at][...]
        vt_all[:, at * own : (at + 1) * own] = v_refs[at][...].T
    for at in range(group):
        q_all[at * own : (at + 1) * own, :] = q_refs[at][...]
    masks = lane_masks()

    def one_query(local_block, carry):
        chunk = local_block // per_own + chunks[0]
        query_block = swap_block(chunk * per_own + local_block % per_own, tensor_at, per_own)
        here = aligned(local_block)
        q_block = q_all[here, :]
        q_heads = [
            q_block[:, spans[head]] * (masks[head % 2] * HD ** (-0.5)).astype(jnp.bfloat16)
            for head in range(heads)
        ]
        low, mid = key_range(info_ref, query_block)

        def one_key(masked, step, state):
            key_block = jnp.where(step < mid, step, query_block) if masked else step
            place = aligned(swap_block(key_block, tensor_at, per_own))
            k_block = k_all[place, :]
            out = []
            if masked:
                allowed = allowed_block(info_ref, key_block, query_block)
            for head in range(heads):
                peak, total, mixed = state[head]
                scores = mm(k_block[:, spans[head]], q_heads[head], NT)
                if masked:
                    scores = jnp.where(allowed, scores, NEG)
                new_peak = jnp.maximum(peak, jnp.max(scores, axis=0, keepdims=True))
                probs = jnp.exp(scores - new_peak)
                decay = jnp.exp(peak - new_peak)
                total = total * decay + jnp.sum(probs, axis=0, keepdims=True)
                v_part = vt_all[pl.ds(head * HD, HD), place]
                mixed = mixed * decay + mm(v_part, probs.astype(jnp.bfloat16))
                out.append((new_peak, total, mixed))
            return tuple(out)

        state = tuple(
            (
                jnp.full((1, BLK), NEG, jnp.float32),
                jnp.zeros((1, BLK), jnp.float32),
                jnp.zeros((HD, BLK), jnp.float32),
            )
            for _ in range(heads)
        )
        state = lax.fori_loop(mid, query_block, functools.partial(one_key, False), state)
        state = lax.fori_loop(low, mid + 1, functools.partial(one_key, True), state)
        both = jnp.concatenate([mixed / total for _, total, mixed in state], axis=0)
        o_all[here, :] = both.T.astype(jnp.bfloat16)
        for head in range(heads):
            peak, total, _ = state[head]
            l_all[pl.ds(head, 1), here] = peak + jnp.log(total)
        return carry

    lax.fori_loop(0, group * per_own, one_query, 0)
    for at in range(group):
        span = slice(at * own, (at + 1) * own)
        o_refs[at][...] = o_all[span, :]
        for head in range(heads):
            l_refs[at][head // 2, pl.ds(head % 2, 1), :] = l_all[pl.ds(head, 1), span]


def attend_forward(info, queries, keys_rot, values, chunks, after=()):
    own, width = queries[0].shape
    count, group = len(keys_rot), len(chunks)
    rows, pairs = own * count, width // PAIR
    together = 1
    wide_pair = together * PAIR
    steps = own * group * rows // 2
    column = pl.BlockSpec((own, wide_pair), lambda p, s: (0, p))
    outs = pl.pallas_call(
        functools.partial(attend_forward_kernel, tuple(chunks), count, own // BLK, len(after)),
        grid_spec=pltpu.PrefetchScalarGridSpec(
            num_scalar_prefetch=1,
            grid=(pairs // together,),
            in_specs=[pl.BlockSpec(memory_space=pl.ANY)] * len(after) + [column] * (group + 2 * count),
            out_specs=[column] * group
            + [pl.BlockSpec((together, 2, own), lambda p, s: (p, 0, 0))] * group,
            scratch_shapes=[
                pltpu.VMEM((group * own, wide_pair), jnp.bfloat16),
                pltpu.VMEM((group * own, wide_pair), jnp.bfloat16),
                pltpu.VMEM((max(2 * together, 8), group * own), jnp.float32),
                pltpu.VMEM((rows, wide_pair), jnp.bfloat16),
                pltpu.VMEM((wide_pair, rows), jnp.bfloat16),
            ],
        ),
        out_shape=[jax.ShapeDtypeStruct((own, width), jnp.bfloat16)] * group
        + [jax.ShapeDtypeStruct((pairs, 2, own), jnp.float32)] * group,
        compiler_params=pltpu.CompilerParams(vmem_limit_bytes=VMEM_LIMIT),
        cost_estimate=spend(
            flops=THRIFT * 16 * steps * width, bytes_accessed=8 * rows * width, transcendentals=steps * width // HD
        ),
        name="attend_forward",
    )(info, *after, *[queries[chunk] for chunk in chunks], *keys_rot, *values)
    return (outs[:group], outs[group:])


def spin(values, cosines, sines_low, sines_high, sign):
    ahead = pltpu.roll(values, PAIR - ROT // 2, 1)
    behind = pltpu.roll(values, ROT // 2, 1)
    return values * cosines + sign * (ahead * sines_low + behind * sines_high)


def attend_backward_kernel(count, pieces, per_own, after, info_ref, *refs):
    do_refs, refs = refs[after : after + pieces], refs[after + pieces :]
    q_refs, k_refs, v_refs, o_refs, l_refs = [
        refs[at * count : (at + 1) * count] for at in range(5)
    ]
    c_ref, sl_ref, sh_ref, out_ref, sum_ref, *scratch = refs[5 * count :]
    q_all, do_all, o_all, l_all, k_all, kt_all, v_all, dk_sum, dv_sum = scratch
    tensor_at = info_ref[2]
    own = per_own * BLK
    heads = k_all.shape[1] // HD
    spans = [slice(head // 2 * PAIR, head // 2 * PAIR + PAIR) for head in range(heads)]
    for at in range(count):
        span = slice(at * own, (at + 1) * own)
        k_all[span, :] = k_refs[at][...]
        kt_all[:, span] = k_refs[at][...].T
        v_all[span, :] = v_refs[at][...]
        q_all[span, :] = q_refs[at][...]
        o_all[span, :] = o_refs[at][...]
        for head in range(heads):
            l_all[pl.ds(head, 1), span] = l_refs[at][head // 2, pl.ds(head % 2, 1), :]
    done = 0
    for one in do_refs:
        do_all[done : done + one.shape[0], :] = one[...]
        done += one.shape[0]
    dk_sum[...] = jnp.zeros_like(dk_sum)
    dv_sum[...] = jnp.zeros_like(dv_sum)
    masks = lane_masks()

    def one_query(local_block, carry):
        query_block = swap_block(local_block, tensor_at, per_own)
        here = aligned(local_block)
        q_block = q_all[here, :]
        do_block = do_all[here, :]
        q_heads = [
            q_block[:, spans[head]] * (masks[head % 2] * HD ** (-0.5)).astype(jnp.bfloat16)
            for head in range(heads)
        ]
        do_heads = [do_block[:, spans[head]] * masks[head % 2] for head in range(heads)]
        prod = (do_block.astype(jnp.float32) * o_all[here, :].astype(jnp.float32)).T
        deltas = [
            jnp.sum(prod[head * HD : (head + 1) * HD], axis=0, keepdims=True) for head in range(heads)
        ]
        logs = [l_all[pl.ds(head, 1), here] for head in range(heads)]
        low, mid = key_range(info_ref, query_block)

        def one_key(masked, step, state):
            key_block = jnp.where(step < mid, step, query_block) if masked else step
            place = aligned(swap_block(key_block, tensor_at, per_own))
            k_block = k_all[place, :]
            v_block = v_all[place, :]
            if masked:
                allowed = allowed_block(info_ref, key_block, query_block)
            out, dk_parts, dv_parts = [], [], []
            for head in range(heads):
                probs = jnp.exp(mm(k_block[:, spans[head]], q_heads[head], NT) - logs[head])
                if masked:
                    probs = jnp.where(allowed, probs, 0.0)
                dprobs = mm(v_block[:, spans[head]], do_heads[head], NT)
                dscores = (probs * (dprobs - deltas[head])).astype(jnp.bfloat16)
                dv_parts.append(mm(probs.astype(jnp.bfloat16), do_heads[head]))
                dk_parts.append(mm(dscores, q_heads[head]))
                out.append(state[head] + mm(kt_all[pl.ds(head * HD, HD), place], dscores))
            for head in range(0, heads, 2):
                dk_sum[place, spans[head]] += dk_parts[head] + dk_parts[head + 1]
                dv_sum[place, spans[head]] += dv_parts[head] + dv_parts[head + 1]
            return tuple(out)

        state = tuple(jnp.zeros((HD, BLK), jnp.float32) for _ in range(heads))
        state = lax.fori_loop(mid, query_block, functools.partial(one_key, False), state)
        state = lax.fori_loop(low, mid + 1, functools.partial(one_key, True), state)
        dq = jnp.concatenate(state, axis=0).T * HD ** (-0.5)
        for span in spans[::2]:
            out_ref[0, here, span] = spin(
                dq[:, span], c_ref[here, :], sl_ref[here, :], sh_ref[here, :], -1.0
            ).astype(jnp.bfloat16)
        return carry

    lax.fori_loop(0, count * per_own, one_query, 0)
    for span in spans[::2]:
        out_ref[1, :, span] = spin(
            dk_sum[:, span], c_ref[...], sl_ref[...], sh_ref[...], -1.0
        ).astype(jnp.bfloat16)
    out_ref[2] = dv_sum[...].astype(jnp.bfloat16)
    for part in range(3):
        sum_ref[pl.ds(part, 1), :] = jnp.sum(
            out_ref[part].astype(jnp.float32), axis=0, keepdims=True
        )


def attend_backward(
    info, queries, keys_rot, values, grad_mix, mixed, logs, tables, first, pairs, held=(), after=()
):
    own, full = queries[0].shape
    count = len(queries)
    rows, width = own * count, pairs * PAIR
    together = 1
    shift = first // together
    steps = rows * rows // 2
    column = pl.BlockSpec((own, together * PAIR), lambda p, s: (0, p + shift))
    line = pl.BlockSpec((together, 2, own), lambda p, s: (p + shift, 0, 0))
    table = pl.BlockSpec((rows, PAIR), lambda p, s: (0, 0))
    far = list(held) + list(after)
    return pl.pallas_call(
        functools.partial(
            attend_backward_kernel, count, len(grad_mix), own // BLK, len(far)
        ),
        grid_spec=pltpu.PrefetchScalarGridSpec(
            num_scalar_prefetch=1,
            grid=(pairs // together,),
            in_specs=[pl.BlockSpec(memory_space=pl.ANY)] * len(far)
            + [
                pl.BlockSpec((one.shape[0], together * PAIR), lambda p, s: (0, p + shift))
                for one in grad_mix
            ]
            + [column] * (4 * count)
            + [line] * count
            + [table] * 3,
            out_specs=[
                pl.BlockSpec((3, rows, together * PAIR), lambda p, s: (0, 0, p + shift)),
                pl.BlockSpec((3, together * PAIR), lambda p, s: (0, p)),
            ],
            scratch_shapes=[
                pltpu.VMEM((rows, together * PAIR), jnp.bfloat16),
                pltpu.VMEM((rows, together * PAIR), jnp.bfloat16),
                pltpu.VMEM((rows, together * PAIR), jnp.bfloat16),
                pltpu.VMEM((max(2 * together, 8), rows), jnp.float32),
                pltpu.VMEM((rows, together * PAIR), jnp.bfloat16),
                pltpu.VMEM((together * PAIR, rows), jnp.bfloat16),
                pltpu.VMEM((rows, together * PAIR), jnp.bfloat16),
                pltpu.VMEM((rows, together * PAIR), jnp.float32),
                pltpu.VMEM((rows, together * PAIR), jnp.float32),
            ],
        ),
        out_shape=[
            jax.ShapeDtypeStruct((3, rows, full), jnp.bfloat16),
            jax.ShapeDtypeStruct((3, width), jnp.float32),
        ],
        input_output_aliases={1: 0} if held else {},
        compiler_params=pltpu.CompilerParams(vmem_limit_bytes=VMEM_LIMIT),
        cost_estimate=spend(
            flops=THRIFT * 40 * steps * width, bytes_accessed=16 * rows * width, transcendentals=steps * width // HD
        ),
        name="attend_backward",
    )(info, *far, *grad_mix, *queries, *keys_rot, *values, *mixed, *logs, *tables)


def project_kernel(x_ref, w_ref, b_ref, c_ref, sl_ref, sh_ref, q_ref, k_ref, v_ref):
    rows_in = x_ref[...]
    width = q_ref.shape[1]
    for part, out_ref in enumerate((q_ref, k_ref, v_ref)):
        full = mm(rows_in, w_ref[part]) + b_ref[pl.ds(part, 1), :]
        if part == 2:
            out_ref[...] = full.astype(jnp.bfloat16)
            continue
        for at in range(0, width, PAIR):
            piece = full[:, at : at + PAIR]
            out_ref[:, at : at + PAIR] = spin(
                piece, c_ref[...], sl_ref[...], sh_ref[...], 1.0
            ).astype(jnp.bfloat16)


def project(normed, weight, bias, tables, chunk=0):
    rows, depth = normed.shape
    width = weight.shape[2]
    block = min(rows, 256)
    first = chunk * rows // block
    table = pl.BlockSpec((block, PAIR), lambda i: (i + first, 0))
    return pl.pallas_call(
        project_kernel,
        grid=(rows // block,),
        in_specs=[
            pl.BlockSpec((block, depth), lambda i: (i, 0)),
            pl.BlockSpec((3, depth, width), lambda i: (0, 0, 0)),
            pl.BlockSpec((3, width), lambda i: (0, 0)),
            table,
            table,
            table,
        ],
        out_specs=[pl.BlockSpec((block, width), lambda i: (i, 0))] * 3,
        out_shape=[jax.ShapeDtypeStruct((rows, width), jnp.bfloat16)] * 3,
        compiler_params=pltpu.CompilerParams(vmem_limit_bytes=VMEM_LIMIT),
        cost_estimate=spend(
            flops=6 * rows * depth * width, bytes_accessed=2 * rows * depth + 6 * (rows + depth) * width, transcendentals=0
        ),
        name="project",
    )(normed, weight, bias, *tables)


def copy_in(source, target, sem):
    made = pltpu.make_async_copy(source, target, sem)
    made.start()
    return made


def feed_kernel(held, split, cut, after, *refs):
    refs = refs[after:]
    x_hbm, dy_hbm, refs = refs[:split], refs[split : split + cut], refs[split + cut :]
    gu_hbm, wd_hbm = refs[:2]
    z_ref, dgu_ref, da_ref = refs[2 + held : 5 + held]
    x_in, dy_in, wg_in, wu_in, wd_in, gate, up, inner_all, sems = refs[5 + held :]
    depth = x_in.shape[1]
    half = depth // 2
    rows = x_in.shape[0]
    piece, slab = rows // split, rows // cut
    get_x = [
        copy_in(x_hbm[at], x_in.at[pl.ds(at * piece, piece)], sems.at[5 + at]) for at in range(split)
    ]
    get_g0 = copy_in(gu_hbm.at[0, pl.ds(0, half)], wg_in.at[pl.ds(0, half)], sems.at[1])
    get_g1 = copy_in(gu_hbm.at[0, pl.ds(half, half)], wg_in.at[pl.ds(half, half)], sems.at[2])
    for one in get_x:
        one.wait()
    get_g0.wait()
    get_u = copy_in(gu_hbm.at[1], wu_in, sems.at[3])
    gate[...] = mm(x_in[:, :half], wg_in[:half])
    get_g1.wait()
    get_dy = [
        copy_in(dy_hbm[at], dy_in.at[pl.ds(at * slab, slab)], sems.at[7 + at])
        for at in range(cut)
    ]
    get_d = copy_in(wd_hbm, wd_in, sems.at[4])
    gate[...] += mm(x_in[:, half:], wg_in[half:])
    get_u.wait()
    up[...] = mm(x_in[...], wu_in[...])
    for one in get_dy:
        one.wait()
    get_d.wait()
    hidden = wd_in.shape[0]
    for at in range(0, hidden, BLK):
        span = slice(at, min(at + BLK, hidden))
        inner_all[:, span] = mm(dy_in[...], wd_in[span, :], NT)
    step = 64

    def middle(at, carry):
        here = pl.ds(pl.multiple_of(at * step, step), step)
        gate_pre, up_pre, inner = gate[here, :], up[here, :], inner_all[here, :]
        sigmoid_gate = 1.0 / (1.0 + jnp.exp(-gate_pre))
        activated = gate_pre * sigmoid_gate
        z_ref[here, :] = (activated * up_pre).astype(jnp.bfloat16)
        dgu_ref[0, here, :] = (
            inner * up_pre * (sigmoid_gate * (1.0 + gate_pre * (1.0 - sigmoid_gate)))
        ).astype(jnp.bfloat16)
        dgu_ref[1, here, :] = (inner * activated).astype(jnp.bfloat16)
        return carry

    lax.fori_loop(0, rows // step, middle, 0)

    def back(at, carry):
        here = pl.ds(pl.multiple_of(at * BLK, BLK), BLK)
        da_ref[:, here] = (
            mm(dgu_ref[0], wg_in[here, :], NT) + mm(dgu_ref[1], wu_in[here, :], NT)
        ).astype(da_ref.dtype)
        return carry

    lax.fori_loop(0, depth // BLK, back, 0)


def feed(chunk, count, normed, back, gate_up, down, held, after=()):
    split, cut = len(normed), len(back)
    rows, depth = normed[0].shape[0] * split, normed[0].shape[1]
    hidden = down.shape[0]
    far = pl.BlockSpec(memory_space=pl.ANY)
    return pl.pallas_call(
        functools.partial(feed_kernel, len(held), split, cut, len(after)),
        grid=(1,),
        in_specs=[far] * (2 + split + cut + len(held) + len(after)),
        out_specs=[
            pl.BlockSpec((rows, hidden), lambda i: (chunk, 0)),
            pl.BlockSpec((2, rows, hidden), lambda i: (0, chunk, 0)),
            pl.BlockSpec((rows, depth), lambda i: (0, 0)),
        ],
        out_shape=[
            jax.ShapeDtypeStruct((rows * count, hidden), jnp.bfloat16),
            jax.ShapeDtypeStruct((2, rows * count, hidden), jnp.bfloat16),
            jax.ShapeDtypeStruct((rows, depth), jnp.float32 if chunk == 0 else jnp.bfloat16),
        ],
        input_output_aliases={len(after) + 2 + split + cut + at: at for at in range(len(held))},
        scratch_shapes=[
            pltpu.VMEM((rows, depth), jnp.bfloat16),
            pltpu.VMEM((rows, depth), jnp.bfloat16),
            pltpu.VMEM((depth, hidden), jnp.bfloat16),
            pltpu.VMEM((depth, hidden), jnp.bfloat16),
            pltpu.VMEM((hidden, depth), jnp.bfloat16),
            pltpu.VMEM((rows, hidden), jnp.float32),
            pltpu.VMEM((rows, hidden), jnp.float32),
            pltpu.VMEM((rows, hidden), jnp.float32),
            pltpu.SemaphoreType.DMA((9,)),
        ],
        compiler_params=pltpu.CompilerParams(vmem_limit_bytes=VMEM_LIMIT),
        cost_estimate=spend(
            flops=10 * rows * depth * hidden, bytes_accessed=6 * depth * hidden, transcendentals=rows * hidden
        ),
        name="feed",
    )(*after, *normed, *back, gate_up, down, *held)


def wide_grad_kernel(count, after, *refs):
    refs = refs[after:]
    lefts, (right, out, turned) = refs[:count], refs[count:]
    done = 0
    for left in lefts:
        turned[:, done : done + left.shape[0]] = left[...].T
        done += left.shape[0]
    for part in range(out.shape[0]):
        out[part] = mm(turned[...], right[part]).astype(jnp.bfloat16)


def wide_grad(lefts, right, after=(), column=0, cuts=1):
    depth = lefts[0].shape[1]
    parts, rows, width = right.shape
    width = width // cuts
    return pl.pallas_call(
        functools.partial(wide_grad_kernel, len(lefts), len(after)),
        grid=(depth // BLK,),
        in_specs=[pl.BlockSpec(memory_space=pl.ANY)] * len(after)
        + [pl.BlockSpec((left.shape[0], BLK), lambda i: (0, i)) for left in lefts]
        + [pl.BlockSpec((parts, rows, width), lambda i: (0, 0, column))],
        out_specs=pl.BlockSpec((parts, BLK, width), lambda i: (0, i, 0)),
        out_shape=jax.ShapeDtypeStruct((parts, depth, width), jnp.bfloat16),
        scratch_shapes=[pltpu.VMEM((BLK, rows), jnp.bfloat16)],
        compiler_params=pltpu.CompilerParams(vmem_limit_bytes=VMEM_LIMIT),
        cost_estimate=spend(
            flops=2 * rows * depth * width * parts,
            bytes_accessed=2 * (rows * depth + parts * width * (rows + depth)),
            transcendentals=0,
        ),
        name="wide_grad",
    )(*after, *lefts, right)


def tall_grad_kernel(held, count, after, *refs):
    refs = refs[after:]
    lefts, rights, (out, turned, joined) = refs[:held], refs[held : held + count], refs[held + count :]
    tall = lefts[0].shape[0]

    @pl.when(pl.program_id(0) == 0)
    def _():
        for at in range(held):
            turned[:, at * tall : (at + 1) * tall] = lefts[at][...].T

    done = 0
    for right in rights:
        joined[done : done + right.shape[0], :] = right[...]
        done += right.shape[0]
    out[...] = mm(turned[...], joined[...]).astype(jnp.bfloat16)


def tall_grad(lefts, rights, after=()):
    tall, depth = lefts[0].shape
    width = rights[0].shape[1]
    count, held = len(rights), len(lefts)
    rows = tall * held
    return pl.pallas_call(
        functools.partial(tall_grad_kernel, held, count, len(after)),
        grid=(width // BLK,),
        in_specs=[pl.BlockSpec(memory_space=pl.ANY)] * len(after)
        + [pl.BlockSpec((tall, depth), lambda i: (0, 0))] * held
        + [pl.BlockSpec((right.shape[0], BLK), lambda i: (0, i)) for right in rights],
        out_specs=pl.BlockSpec((depth, BLK), lambda i: (0, i)),
        out_shape=jax.ShapeDtypeStruct((depth, width), jnp.bfloat16),
        scratch_shapes=[
            pltpu.VMEM((depth, rows), jnp.bfloat16),
            pltpu.VMEM((rows, BLK), jnp.bfloat16),
        ],
        compiler_params=pltpu.CompilerParams(vmem_limit_bytes=VMEM_LIMIT),
        cost_estimate=spend(
            flops=2 * rows * depth * width,
            bytes_accessed=2 * (rows * depth + width * (rows + depth)),
            transcendentals=0,
        ),
        name="tall_grad",
    )(*after, *lefts, *rights)


FAR = pl.BlockSpec(memory_space=pl.ANY)


def halves_kernel(after, count, *refs):
    for source, target in zip(refs[after : after + count], refs[after + count :]):
        target[...] = source[...]


def halves(picks, after=()):
    half, depth = picks[0][0].shape[0] // 2, picks[0][0].shape[1]
    specs = [
        pl.BlockSpec((half, depth), functools.partial(lambda which, i: (which, 0), which))
        for _, which in picks
    ]
    return pl.pallas_call(
        functools.partial(halves_kernel, len(after), len(picks)),
        grid=(1,),
        in_specs=[FAR] * len(after) + specs,
        out_specs=[pl.BlockSpec((half, depth), lambda i: (0, 0))] * len(picks),
        out_shape=[jax.ShapeDtypeStruct((half, depth), picks[0][0].dtype)] * len(picks),
        compiler_params=pltpu.CompilerParams(vmem_limit_bytes=VMEM_LIMIT),
        cost_estimate=spend(
            flops=half * depth, bytes_accessed=4 * len(picks) * half * depth, transcendentals=0
        ),
        name="halves",
    )(*after, *[one for one, _ in picks])


def join_kernel(after, *refs):
    top, end, out = refs[after:]
    half = top.shape[0]
    out[:half, :] = top[...]
    out[half:, :] = end[...]


def join(top, end, after=()):
    half, depth = top.shape
    whole = pl.BlockSpec((half, depth), lambda i: (0, 0))
    return pl.pallas_call(
        functools.partial(join_kernel, len(after)),
        grid=(1,),
        in_specs=[FAR] * len(after) + [whole, whole],
        out_specs=pl.BlockSpec((2 * half, depth), lambda i: (0, 0)),
        out_shape=jax.ShapeDtypeStruct((2 * half, depth), top.dtype),
        compiler_params=pltpu.CompilerParams(vmem_limit_bytes=VMEM_LIMIT),
        cost_estimate=spend(flops=half * depth, bytes_accessed=8 * half * depth, transcendentals=0),
        name="join",
    )(*after, top, end)


def shrink_kernel(after, *refs):
    source, scale, out = refs[after:]
    out[...] = (source[...].astype(jnp.float32) * scale[...]).astype(jnp.bfloat16)


def shrink(values, scale, after=()):
    rows, depth = values.shape
    block = rows // 4
    return pl.pallas_call(
        functools.partial(shrink_kernel, len(after)),
        grid=(4,),
        in_specs=[FAR] * len(after)
        + [
            pl.BlockSpec((block, depth), lambda i: (i, 0)),
            pl.BlockSpec((block, 1), lambda i: (i, 0)),
        ],
        out_specs=pl.BlockSpec((block, depth), lambda i: (i, 0)),
        out_shape=jax.ShapeDtypeStruct((rows, depth), jnp.bfloat16),
        compiler_params=pltpu.CompilerParams(vmem_limit_bytes=VMEM_LIMIT),
        cost_estimate=spend(
            flops=rows * depth, bytes_accessed=6 * rows * depth, transcendentals=0
        ),
        name="shrink",
    )(*after, values, scale)


LINES = 128


def arrived(own, parts, steps):
    total = own[...].astype(jnp.float32)
    if parts:
        first = pl.program_id(0) < steps // 2
        one, two, three, four = [part[...].astype(jnp.float32) for part in parts]
        total = total + jnp.where(first, one + two, three + four)
    return total


def part_specs(parts, depth, steps):
    if not parts:
        return []
    top = pl.BlockSpec((LINES, depth), lambda i: (jnp.minimum(i, steps // 2 - 1), 0))
    end = pl.BlockSpec((LINES, depth), lambda i: (jnp.maximum(i - steps // 2, 0), 0))
    return [top, top, end, end]


def unit_of(values):
    average = jnp.mean(values, axis=-1, keepdims=True)
    centered = values - average
    inverse = lax.rsqrt(jnp.mean(centered * centered, axis=-1, keepdims=True) + NORM_EPS)
    return (centered * inverse, inverse)


def settle_kernel(held, after, steps, *refs):
    refs = refs[after:]
    own, parts = refs[0], refs[1 : 1 + held]
    resid, gain, shift, hidden, normed = refs[1 + held :]
    values = resid[...].astype(jnp.float32) + arrived(own, parts, steps)
    hidden[...] = values
    normed[...] = (unit_of(values)[0] * gain[...] + shift[...]).astype(jnp.bfloat16)


def settle(own, parts, resid, gain, shift, after=()):
    rows, depth = own.shape
    steps = rows // LINES
    block = pl.BlockSpec((LINES, depth), lambda i: (i, 0))
    line = pl.BlockSpec((1, depth), lambda i: (0, 0))
    return pl.pallas_call(
        functools.partial(settle_kernel, len(parts), len(after), steps),
        grid=(steps,),
        in_specs=[FAR] * len(after)
        + [block]
        + part_specs(parts, depth, steps)
        + [block, line, line],
        out_specs=[block, block],
        out_shape=[
            jax.ShapeDtypeStruct((rows, depth), jnp.float32),
            jax.ShapeDtypeStruct((rows, depth), jnp.bfloat16),
        ],
        compiler_params=pltpu.CompilerParams(vmem_limit_bytes=VMEM_LIMIT),
        cost_estimate=spend(
            flops=10 * rows * depth, bytes_accessed=16 * rows * depth, transcendentals=rows
        ),
        name="settle",
    )(*after, own, *parts, resid, gain, shift)


def finish_kernel(held, after, steps, *refs):
    refs = refs[after:]
    own, parts = refs[0], refs[1 : 1 + held]
    hidden, out = refs[1 + held :]
    total = hidden[...] + arrived(own, parts, steps)
    out[...] = total.astype(jnp.bfloat16)


def finish(own, parts, hidden, after=()):
    rows, depth = own.shape
    steps = rows // LINES
    block = pl.BlockSpec((LINES, depth), lambda i: (i, 0))
    return pl.pallas_call(
        functools.partial(finish_kernel, len(parts), len(after), steps),
        grid=(steps,),
        in_specs=[FAR] * len(after) + [block] + part_specs(parts, depth, steps) + [block],
        out_specs=block,
        out_shape=jax.ShapeDtypeStruct((rows, depth), jnp.bfloat16),
        compiler_params=pltpu.CompilerParams(vmem_limit_bytes=VMEM_LIMIT),
        cost_estimate=spend(
            flops=4 * rows * depth, bytes_accessed=12 * rows * depth, transcendentals=0
        ),
        name="finish",
    )(*after, own, *parts, hidden)


def unsettle_kernel(held, after, steps, *refs):
    refs = refs[after:]
    own, parts = refs[0], refs[1 : 1 + held]
    values, extra, gain, total, short, gain_sum, shift_sum = refs[1 + held :]
    incoming = arrived(own, parts, steps)
    unit_rows, inverse = unit_of(values[...].astype(jnp.float32))
    scaled = incoming * gain[...]
    grad_rows = inverse * (
        scaled
        - jnp.mean(scaled, axis=-1, keepdims=True)
        - unit_rows * jnp.mean(scaled * unit_rows, axis=-1, keepdims=True)
    )
    result = extra[...].astype(jnp.float32) + grad_rows
    total[...] = result
    short[...] = result.astype(jnp.bfloat16)

    @pl.when(pl.program_id(0) == 0)
    def _():
        gain_sum[...] = jnp.zeros_like(gain_sum)
        shift_sum[...] = jnp.zeros_like(shift_sum)

    gain_sum[...] += jnp.sum(incoming * unit_rows, axis=0, keepdims=True)
    shift_sum[...] += jnp.sum(incoming, axis=0, keepdims=True)


def unsettle(own, parts, values, extra, gain, after=()):
    rows, depth = own.shape
    steps = rows // LINES
    block = pl.BlockSpec((LINES, depth), lambda i: (i, 0))
    line = pl.BlockSpec((1, depth), lambda i: (0, 0))
    return pl.pallas_call(
        functools.partial(unsettle_kernel, len(parts), len(after), steps),
        grid=(steps,),
        in_specs=[FAR] * len(after)
        + [block]
        + part_specs(parts, depth, steps)
        + [block, block, line],
        out_specs=[block, block, line, line],
        out_shape=[
            jax.ShapeDtypeStruct((rows, depth), jnp.float32),
            jax.ShapeDtypeStruct((rows, depth), jnp.bfloat16),
            jax.ShapeDtypeStruct((1, depth), jnp.float32),
            jax.ShapeDtypeStruct((1, depth), jnp.float32),
        ],
        compiler_params=pltpu.CompilerParams(vmem_limit_bytes=VMEM_LIMIT),
        cost_estimate=spend(
            flops=20 * rows * depth, bytes_accessed=20 * rows * depth, transcendentals=rows
        ),
        name="unsettle",
    )(*after, own, *parts, values, extra, gain)


def unproject_kernel(count, after, *refs):
    refs = refs[after:]
    lefts, w_ref, outs = refs[:count], refs[count], refs[count + 1 :]
    own = outs[0].shape[0]
    total = None
    for part in range(3):
        left = jnp.concatenate([one[part] for one in lefts], axis=0)
        made = mm(left, w_ref[part], NT)
        total = made if total is None else total + made
    for at, out in enumerate(outs):
        out[...] = total[at * own : (at + 1) * own].astype(out.dtype)


def unproject(grads, weight, chunks, own, after=()):
    parts, depth, width = weight.shape
    count = len(chunks)
    return pl.pallas_call(
        functools.partial(unproject_kernel, count, len(after)),
        grid=(depth // BLK,),
        in_specs=[FAR] * len(after)
        + [
            pl.BlockSpec((parts, own, width), functools.partial(lambda which, i: (0, which, 0), chunk))
            for chunk in chunks
        ]
        + [pl.BlockSpec((parts, BLK, width), lambda i: (0, i, 0))],
        out_specs=[pl.BlockSpec((own, BLK), lambda i: (0, i))] * count,
        out_shape=[
            jax.ShapeDtypeStruct((own, depth), jnp.bfloat16 if chunk else jnp.float32)
            for chunk in chunks
        ],
        compiler_params=pltpu.CompilerParams(vmem_limit_bytes=VMEM_LIMIT),
        cost_estimate=spend(
            flops=2 * parts * own * count * depth * width,
            bytes_accessed=2 * parts * width * (own * count + depth) + 4 * own * count * depth,
            transcendentals=0,
        ),
        name="unproject",
    )(*after, *[grads] * count, weight)


def adam_kernel(rate, decay, after, *refs):
    weight, gradient, first, second, grad_out, first_out, second_out, weight_out = refs[after:]
    grad = gradient[...].astype(jnp.float32)
    grad_out[...] = grad
    first_out[...], second_out[...], weight_out[...] = adam_update(
        weight[...], grad, first[...], second[...], rate, decay
    )


def adam(weight, gradient, first, second, rate, after=()):
    shape = weight.shape
    flat = (-1, shape[-1])
    arrays = [one.reshape(flat) for one in (weight, gradient, first, second)]
    rows, width = arrays[0].shape
    block = pl.BlockSpec((rows // 4, width), lambda i: (i, 0))
    outs = pl.pallas_call(
        functools.partial(adam_kernel, rate, WEIGHT_DECAY, len(after)),
        grid=(4,),
        in_specs=[FAR] * len(after) + [block] * 4,
        out_specs=[block] * 4,
        out_shape=[jax.ShapeDtypeStruct((rows, width), jnp.float32)] * 4,
        compiler_params=pltpu.CompilerParams(vmem_limit_bytes=VMEM_LIMIT),
        cost_estimate=spend(
            flops=12 * rows * width, bytes_accessed=30 * rows * width, transcendentals=0
        ),
        name="adam",
    )(*after, *arrays)
    return [one.reshape(shape) for one in outs]


def hold(values, after):
    rows, depth = values.shape
    whole = pl.BlockSpec((rows, depth), lambda i: (0, 0))

    def body(*refs):
        refs[-1][...] = refs[-2][...]

    return pl.pallas_call(
        body,
        grid=(1,),
        in_specs=[FAR] * len(after) + [whole],
        out_specs=whole,
        out_shape=jax.ShapeDtypeStruct((rows, depth), values.dtype),
        cost_estimate=spend(
            flops=rows * depth, bytes_accessed=8 * rows * depth, transcendentals=0
        ),
        name="hold",
    )(*after, values)


def first_line_kernel(after, *refs):
    w_ref, first_ref, second_ref, sum_ref, out_ref = refs[after:]
    cut = first_ref.shape[2]
    gain, shift = None, None
    for part in range(3):
        weight = w_ref[part].astype(jnp.float32)
        grad = jnp.concatenate([first_ref[part], second_ref[part]], axis=1).astype(jnp.float32)
        gain = weight * grad if gain is None else gain + weight * grad
        lean = weight * sum_ref[pl.ds(part, 1), :]
        shift = lean if shift is None else shift + lean
    out_ref[pl.ds(0, 1), :] = jnp.sum(gain.T, axis=0, keepdims=True)
    out_ref[pl.ds(1, 1), :] = jnp.sum(shift.T, axis=0, keepdims=True)


def first_line(weight, first, second, sums, after):
    parts, depth, width = weight.shape
    cut = first.shape[2]
    return pl.pallas_call(
        functools.partial(first_line_kernel, len(after)),
        grid=(depth // BLK,),
        in_specs=[FAR] * len(after)
        + [
            pl.BlockSpec((parts, BLK, width), lambda i: (0, i, 0)),
            pl.BlockSpec((parts, BLK, cut), lambda i: (0, i, 0)),
            pl.BlockSpec((parts, BLK, width - cut), lambda i: (0, i, 0)),
            pl.BlockSpec((parts, width), lambda i: (0, 0)),
        ],
        out_specs=pl.BlockSpec((2, BLK), lambda i: (0, i)),
        out_shape=jax.ShapeDtypeStruct((2, depth), jnp.float32),
        compiler_params=pltpu.CompilerParams(vmem_limit_bytes=VMEM_LIMIT),
        cost_estimate=spend(
            flops=4 * parts * depth * width, bytes_accessed=4 * parts * depth * width, transcendentals=0
        ),
        name="first_line",
    )(*after, weight, first, second, sums)


def down_project_kernel(after, count, *refs):
    z_ref, w_ref, outs = refs[after], refs[after + 1], refs[after + 2 :]
    for at in range(count):

        @pl.when(pl.program_id(0) == at)
        def _():
            outs[at][...] = mm(z_ref[...], w_ref[...]).astype(jnp.bfloat16)


def down_project(inner, weight, count, after=()):
    rows, hidden = inner.shape
    depth = weight.shape[1]
    own = rows // count
    return pl.pallas_call(
        functools.partial(down_project_kernel, len(after), count),
        grid=(count,),
        in_specs=[FAR] * len(after)
        + [
            pl.BlockSpec((own, hidden), lambda i: (i, 0)),
            pl.BlockSpec((hidden, depth), lambda i: (0, 0)),
        ],
        out_specs=[pl.BlockSpec((own, depth), lambda i: (0, 0))] * count,
        out_shape=[jax.ShapeDtypeStruct((own, depth), jnp.bfloat16)] * count,
        compiler_params=pltpu.CompilerParams(vmem_limit_bytes=VMEM_LIMIT),
        cost_estimate=spend(
            flops=2 * rows * depth * hidden,
            bytes_accessed=2 * (rows * depth + hidden * (rows + depth)),
            transcendentals=0,
        ),
        name="down_project",
    )(*after, inner, weight)


def lane_tables(position):
    half_rot = ROT // 2
    lane = jnp.arange(PAIR, dtype=jnp.int32) % HD
    freqs = 10000.0 ** (-((lane % half_rot).astype(jnp.float32) * (2.0 / ROT)))
    angles = position.astype(jnp.float32)[:, None] * freqs[None, :]
    cosines, sines = jnp.cos(angles), jnp.sin(angles)
    in_low, in_high = (lane < half_rot)[None], ((lane >= half_rot) & (lane < ROT))[None]
    return (
        jnp.where((lane < ROT)[None], cosines, 1.0),
        jnp.where(in_low, -sines, 0.0),
        jnp.where(in_high, sines, 0.0),
    )


def sequence_facts(lengths, owners, dp_index):
    owned = owners == dp_index
    total = jnp.sum(jnp.where(owned, lengths, 0))
    return (lengths[jnp.argmax(owned)], total)


def norm_forward(values, gain, shift):
    return unit_of(values)[0] * gain + shift


def adam_update(weight_old, gradient, first_old, second_old, rate, decay):
    first_new = BETA_ONE * first_old + (1.0 - BETA_ONE) * gradient
    second_new = BETA_TWO * second_old + (1.0 - BETA_TWO) * gradient * gradient
    first_hat = first_new / (1.0 - BETA_ONE**STEP)
    second_hat = second_new / (1.0 - BETA_TWO**STEP)
    weight_new = weight_old * (1.0 - rate * decay) - rate * first_hat / (
        jnp.sqrt(second_hat) + ADAM_EPS
    )
    return (first_new, second_new, weight_new)


def low(values):
    return values.astype(jnp.bfloat16)


def wide(values):
    return values.astype(jnp.float32)


def swap(values, axis, bits):
    size = lax.axis_size(axis)
    return lax.ppermute(values, axis, [(at, at ^ bits) for at in range(size)])


def gather_start(rows):
    count = lax.axis_size("tensor")
    if count != 4:
        return [swap(rows, "tensor", bits) for bits in range(1, count)]
    return [swap(rows, "tensor", 1), swap(rows, "tensor", 2)]


def gather_on(near, after=(), with_sends=False):
    passed, sends = (), ()
    if lax.axis_size("tensor") == 4:
        sends = halves([(near[0], 0), (near[1], 1)], after)
        passed = (swap(sends[0], "tensor", 2), swap(sends[1], "tensor", 1))
    return (passed, sends) if with_sends else passed


def pieces_of(pieces, chunk):
    return pieces[3:] if len(pieces) == 5 and chunk == 3 else [pieces[chunk]]


def scatter_start(parts, after=()):
    if lax.axis_size("tensor") != 4:
        return [swap(low(parts[bits]), "tensor", bits) for bits in range(1, len(parts))]
    _, one, two, three = parts
    half = one.shape[0] // 2
    if after:
        three_top, three_end, one_top, two_end = after
    else:
        three = low(three)
        three_top, three_end = three[:half], three[half:]
        one_top, two_end = low(one[:half]), low(two[half:])
    return [
        swap(three_top, "tensor", 1),
        swap(three_end, "tensor", 2),
        swap(one_top, "tensor", 1),
        swap(two_end, "tensor", 2),
    ]


def scatter_on(parts, moved):
    if lax.axis_size("tensor") != 4:
        return []
    _, one, two, _ = parts
    half = one.shape[0] // 2
    return [low(wide(one[half:]) + wide(moved[1])), low(wide(two[:half]) + wide(moved[0]))]


def scatter_end(parts, moved, passing=None):
    if lax.axis_size("tensor") != 4:
        total = wide(parts[0])
        for one in moved:
            total = total + wide(one)
        return (total, [])
    one_end, two_top = passing or scatter_on(parts, moved)
    return (
        parts[0],
        [moved[2], swap(two_top, "tensor", 2), swap(one_end, "tensor", 1), moved[3]],
    )


def sum_along(values, axis):
    bits = 1
    while bits < lax.axis_size(axis):
        values = values + swap(values, axis, bits)
        bits *= 2
    return values


def scatter_weight(partial):
    return lax.psum_scatter(partial, "dp", scatter_dimension=1, tiled=True)


def dot(left, right, dims):
    return lax.dot_general(left, right, (dims, ((), ())), preferred_element_type=jnp.float32)


def local(
    hidden_in,
    grad_out,
    lengths,
    owners,
    qkv_weight,
    out_weight,
    gate_up_weight,
    down_weight,
    norm_gain,
    norm_bias,
    qkv_bias,
    qkv_first,
    out_first,
    gate_up_first,
    down_first,
    small_first,
    qkv_second,
    out_second,
    gate_up_second,
    down_second,
    small_second,
):
    dp_index = lax.axis_index("dp")
    tp_index = lax.axis_index("tensor")
    count = lax.axis_size("tensor")
    own_rows = hidden_in.shape[0]
    local_width = qkv_weight.shape[2]
    chunks = list(range(count))
    groups = [[3], [1, 2], [0]] if count == 4 else [chunks[1:], [0]]
    qkv_full, out_full, gate_up_full, down_full = [
        lax.all_gather(low(one), "dp", axis=1, tiled=True)
        for one in (qkv_weight, out_weight, gate_up_weight, down_weight)
    ]
    split, total = sequence_facts(lengths, owners, dp_index)
    row_ids = jnp.concatenate(
        [(tp_index ^ chunk) * own_rows + jnp.arange(own_rows, dtype=jnp.int32) for chunk in chunks]
    )
    starts = jnp.where(row_ids < split, 0, jnp.where(row_ids < total, split, total))
    live_own = wide(row_ids[:own_rows] < total)
    info = jnp.stack([split, total, tp_index, tp_index]).astype(jnp.int32)
    lanes = lane_tables(row_ids - starts)
    bias_local = lax.dynamic_slice_in_dim(qkv_bias, tp_index * local_width, local_width, 1)

    first_norm = low(norm_forward(wide(hidden_in), norm_gain[0], norm_bias[0]))
    near = gather_start(first_norm)
    passed = gather_on(near)
    early = [
        project(one, qkv_full, bias_local, lanes, chunk)
        for chunk, one in enumerate([first_norm] + near)
    ]
    normed_one = [first_norm] + near
    if passed:
        normed_one.append(join(*passed, [one[0] for one in early]))
    projected = early + [
        project(normed_one[chunk], qkv_full, bias_local, lanes, chunk)
        for chunk in chunks[len(early) :]
    ]
    queries, keys_rot, values = [[one[part] for one in projected] for part in range(3)]
    cotangent = shrink(grad_out, live_own[:, None], normed_one[1:])
    near = gather_start(cotangent)
    passed = gather_on(near)
    back_ffn = [cotangent, *near] + ([join(*passed)] if passed else [])

    attn_mix, log_total = [None] * count, [None] * count
    for step, group in enumerate(groups):
        after = near if step == 1 else ()
        mixed, logs = attend_forward(info, queries, keys_rot, values, group, after)
        for at, chunk in enumerate(group):
            attn_mix[chunk], log_total[chunk] = mixed[at], logs[at]
    parts = [dot(one, out_full, ((1,), (0,))) for one in attn_mix]
    hidden, second_norm = settle(
        *scatter_end(parts, scatter_start(parts)),
        hidden_in,
        norm_gain[1:2],
        norm_bias[1:2],
    )

    near = gather_start(second_norm)
    held, back_second = (), [None] * count

    def feed_one(chunk, normed, held, after=()):
        *held, back_second[chunk] = feed(
            chunk, count, normed, pieces_of(back_ffn, chunk), gate_up_full, down_full, held, after
        )
        return held

    held = feed_one(0, [second_norm], held)
    passed = gather_on(near, held[:1])
    held = feed_one(1, near[:1], held)
    normed_two = [second_norm, *near, *passed]
    for chunk in [3, 2] if count == 4 else chunks[2:]:
        held = feed_one(chunk, pieces_of(normed_two, chunk), held)
    inner_act, grad_gate_up = held
    moved = scatter_start(back_second)
    passing = scatter_on(back_second, moved)
    gate_up_partial = wide_grad(normed_two, grad_gate_up, moved[:2] + passing)
    gate_up_grad = scatter_weight(gate_up_partial)
    layer_parts = down_project(inner_act, down_full, count, [gate_up_partial])
    grad_hidden, grad_hidden_low, gain_two_grad, bias_two_grad = unsettle(
        *scatter_end(back_second, moved, passing),
        hidden,
        cotangent,
        norm_gain[1:2],
        [gate_up_partial, *layer_parts],
    )
    near = gather_start(grad_hidden_low)
    down_partial = tall_grad([inner_act], back_ffn, [grad_hidden_low])
    down_grad = scatter_weight(down_partial)
    passed = gather_on(near, [down_partial])
    back_attn = [grad_hidden_low, *near, *passed]

    grad_mix = [low(dot(one, out_full, ((1,), (1,)))) for one in back_attn]
    layer_sends = []
    if count == 4:
        layer_sends = halves(
            [(layer_parts[3], 0), (layer_parts[3], 1), (layer_parts[1], 0), (layer_parts[2], 1)],
            back_attn[1:],
        )
    layer_moved = scatter_start(layer_parts, layer_sends)
    pairs = local_width // PAIR
    cut = pairs // 2
    saved = (info, queries, keys_rot, values, grad_mix, attn_mix, log_total, lanes)
    first_proj, first_sums = attend_backward(*saved, 0, cut, (), [gate_up_grad] + layer_moved[:2])
    first_partial = wide_grad(normed_one, first_proj, (), 0, 2)
    first_grad = scatter_weight(first_partial)
    out_partial = tall_grad(attn_mix, back_attn, [first_partial])
    out_grad = scatter_weight(out_partial)
    passing = scatter_on(layer_parts, layer_moved)
    grad_proj, second_sums = attend_backward(
        *saved, cut, pairs - cut, [first_proj], [out_partial] + passing
    )
    layer_own, layer_rest = scatter_end(layer_parts, layer_moved, passing)
    second_partial = wide_grad(
        normed_one, grad_proj, [first_grad] + layer_rest, 1, 2
    )
    parts = unproject(grad_proj, qkv_full, chunks, own_rows, [second_partial])
    moved = scatter_start(parts)
    onward = scatter_on(parts, moved)
    settled = scatter_end(parts, moved, onward)
    layer_out = finish(layer_own, layer_rest, hidden, parts[1:])
    second_grad = scatter_weight(second_partial)
    qkv_grad = wide(jnp.concatenate([first_grad, second_grad], axis=2))
    out_grad, gate_up_grad, down_grad = wide(out_grad), wide(gate_up_grad), wide(down_grad)
    input_grad = unsettle(
        *settled, hidden_in, grad_hidden, norm_gain[:1], [second_grad]
    )[0]

    bias_local_grad = jnp.concatenate([first_sums, second_sums], axis=1)
    lines = first_line(qkv_full, first_partial, second_partial, bias_local_grad, parts[1:])
    gain_one_grad = (lines[:1] - norm_bias[:1] * lines[1:]) / norm_gain[:1]
    bias_grad_full = lax.dynamic_update_slice_in_dim(
        jnp.zeros((3, qkv_bias.shape[1]), jnp.float32), bias_local_grad, tp_index * local_width, 1
    )
    small_grad = jnp.concatenate(
        [gain_one_grad, gain_two_grad, lines[1:], bias_two_grad, bias_grad_full], axis=0
    )
    small_weight = jnp.concatenate([norm_gain, norm_bias, qkv_bias], axis=0)
    qkv_first_new, qkv_second_new, qkv_new = adam_update(
        qkv_weight, qkv_grad, qkv_first, qkv_second, RATE_QKV, WEIGHT_DECAY
    )
    out_first_new, out_second_new, out_new = adam_update(
        out_weight, out_grad, out_first, out_second, RATE_OUT, WEIGHT_DECAY
    )
    gate_up_first_new, gate_up_second_new, gate_up_new = adam_update(
        gate_up_weight, gate_up_grad, gate_up_first, gate_up_second, RATE_GATE_UP, WEIGHT_DECAY
    )
    down_first_new, down_second_new, down_new = adam_update(
        down_weight, down_grad, down_first, down_second, RATE_DOWN, WEIGHT_DECAY
    )
    settled_all = list(settled[1]) + [layer_out, down_new, gate_up_new, out_new, qkv_new]
    small_grad = sum_along(sum_along(hold(small_grad, settled_all), "tensor"), "dp")
    small_first_new, small_second_new, small_new = adam_update(
        small_weight, small_grad, small_first, small_second, RATE_SMALL, 0.0
    )
    return (
        layer_out,
        input_grad,
        qkv_grad,
        qkv_first_new,
        qkv_second_new,
        qkv_new,
        out_grad,
        out_first_new,
        out_second_new,
        out_new,
        gate_up_grad,
        gate_up_first_new,
        gate_up_second_new,
        gate_up_new,
        down_grad,
        down_first_new,
        down_second_new,
        down_new,
        small_grad,
        small_first_new,
        small_second_new,
        small_new,
    )


def solution(mesh):
    placed = (
        P(("dp", "tensor"), None),
        P(("dp", "tensor"), None),
        P(),
        P(),
        P(None, "dp", "tensor"),
        P("tensor", "dp"),
        P(None, "dp", "tensor"),
        P("tensor", "dp"),
        P(),
        P(),
        P(),
        P(None, "dp", "tensor"),
        P("tensor", "dp"),
        P(None, "dp", "tensor"),
        P("tensor", "dp"),
        P(),
        P(None, "dp", "tensor"),
        P("tensor", "dp"),
        P(None, "dp", "tensor"),
        P("tensor", "dp"),
        P(),
    )
    return jax.shard_map(
        local,
        mesh=mesh,
        in_specs=placed,
        out_specs=(
            P(("dp", "tensor"), None),
            P(("dp", "tensor"), None),
            P(None, "dp", "tensor"),
            P(None, "dp", "tensor"),
            P(None, "dp", "tensor"),
            P(None, "dp", "tensor"),
            P("tensor", "dp"),
            P("tensor", "dp"),
            P("tensor", "dp"),
            P("tensor", "dp"),
            P(None, "dp", "tensor"),
            P(None, "dp", "tensor"),
            P(None, "dp", "tensor"),
            P(None, "dp", "tensor"),
            P("tensor", "dp"),
            P("tensor", "dp"),
            P("tensor", "dp"),
            P("tensor", "dp"),
            P(),
            P(),
            P(),
            P(),
        ),
        check_vma=False,
    )
```

time: 2460 us -> 932 us (0.38)
  waiting for transfers between devices: 1130 us -> 204 us
  matrix products: 924 us -> 22.4 us
  Pallas kernels: 0 us -> 522 us
  local copies, waits for them, and re-layouts: 185 us -> 23.2 us
  other arithmetic: 149 us -> 57.6 us
  starting transfers between devices: 0.67 us -> 76.4 us
  blocking collectives: 39.6 us -> 0 us
    dot_general x40 -> x9, matrix products: 924 us -> 22.4 us  [dot(): lax.dot_general(left, right, (dims, ((), ())), preferred_element_type=jnp...]
    reduce_scatter x8 -> x5, waiting for transfers between devices: 635 us -> 59 us  [scatter_weight(): return lax.psum_scatter(partial, 'dp', scatter_dimension=1, tiled=True)]
    pallas_call x0 -> x34, Pallas kernels: none -> 522 us  [the longest x4 100 us: feed(): pl.pallas_call(functools.partial(feed_kernel, len(held), split, cut, len(...]
    all_gather x8 -> x4, waiting for transfers between devices: 490 us -> 0.02 us  [local(): lax.all_gather(low(one), 'dp', axis=1, tiled=True)]
    ppermute x0 -> x45, waiting for transfers between devices: none -> 144 us  [swap(): return lax.ppermute(values, axis, [(at, at ^ bits) for at in range(size)])]
    dynamic_update_slice x8 -> x0, local copies, waits for them, and re-layouts: 93.4 us -> none  [attend_backward(): lax.scan(one_block, (zeros_heads, zeros_heads), jnp.arange(CAP // block_r...]
    ppermute x0 -> x45, starting transfers between devices: none -> 76.1 us  [swap(): return lax.ppermute(values, axis, [(at, at ^ bits) for at in range(size)])]
    reduce_sum x12 -> x3, other arithmetic: 77.1 us -> 1.67 us  [the longest x1 0.69 us: unit_of(): jnp.mean(centered * centered, axis=-1, keepdims=True) + NORM_EPS]
  transfers between devices with their start and end apart: 16 -> 54, of which waited for: 12 -> 19; matrix products, arithmetic and copies ran while one was open for 47% -> 10% of each run, Pallas kernels for 0% -> 43%
where the time goes in v1:
time: 932 us; the launch traced here: 922 us
  Pallas kernels  522 us (56%)
  waiting for transfers between devices  204 us (22%)
  starting transfers between devices  76.4 us (8%)
  other arithmetic  57.6 us (6%)
  local copies, waits for them, and re-layouts  23.2 us (2%)
  matrix products  22.4 us (2%)
  between operations  16.9 us (2%)
    ppermute x45, waiting for transfers between devices, swap(): return lax.ppermute(values, axis, [(at, at ^ bits) for at in range(size)])  144 us
    pallas_call x4, Pallas kernels, feed(): pl.pallas_call(functools.partial(feed_kernel, len(held), split, cut, len(...  100 us
    pallas_call x2, Pallas kernels, attend_backward(): pl.pallas_call(functools.partial(attend_backward_kernel, count, len(grad_...  98.2 us
    pallas_call x3, Pallas kernels, attend_forward(): pl.pallas_call(functools.partial(attend_forward_kernel, tuple(chunks), co...  91.1 us
    ppermute x45, starting transfers between devices, swap(): return lax.ppermute(values, axis, [(at, at ^ bits) for at in range(size)])  76.1 us
    pallas_call x3, Pallas kernels, wide_grad(): pl.pallas_call(functools.partial(wide_grad_kernel, len(lefts), len(after)...  59.2 us
    reduce_scatter x5, waiting for transfers between devices, scatter_weight(): return lax.psum_scatter(partial, 'dp', scatter_dimension=1, tiled=True)  59 us
    pallas_call x4, Pallas kernels, project(): pl.pallas_call(project_kernel, grid=(rows // block,), in_specs=[pl.BlockS...  31 us
  transfers between devices with their start and end apart: 54, of which 19 were waited for; matrix products, arithmetic and copies ran while one was open for 10% of the time, Pallas kernels for 43%

profile of v1, /device:TPU:0, one launch (start us, length us, event | category | flops | bytes accessed | tf_op | source)
XLA Modules:
  0.0 922.4 jit_solution(8830545586733648666)
XLA Ops:
  35.1 33.2 %collective-permute-done.1.x_ref.refs_1_.refs_2_.refs_7_ = bf16[512,2048]{1,0:T(8,128)(2,1)S(1)} collective-permute-done((bf16[512,2048]{1,0:T(8,128)(2,1)}, bf16[512,2048]{1,0:T(8,128)(2,1)S(1)}, u32[]{:S(2)}, u32[]{:S(2)}) %collective-permute-start.1) | collective-permute-done | bytes 2097184 | tf_op jit(solution)/shard_map/ppermute | solution.py:989
  86.1 7.8 project.5
  114.2 7.9 project.7
  122.1 36.4 %attend_forward.5 = (bf16[512,512]{1,0:T(8,128)(2,1)}, f32[4,2,512]{2,1,0:T(2,128)}) custom-call(s32[4]{0:T(128)} %pad_add_fusion.1.info_ref, bf16[512,512]{1,0:T(8,128)(2,1)} %get-tuple-element.103.refs_0_.refs_11_.refs_12_, bf16[512,512]{1,0:T(8,128)(2,1)} %get-tuple-element.92.refs_1_.refs_4_.refs_12_.refs_13_, ...), custom_call_target="tpu_custom_call" | custom-call | flops 4294967296 | bytes 8388608 | tf_op jit(solution)/shard_map/attend_forward/pallas_call | solution.py:163
  161.9 41.1 %attend_forward.4 = (bf16[512,512]{1,0:T(8,128)(2,1)}, bf16[512,512]{1,0:T(8,128)(2,1)}, f32[4,2,512]{2,1,0:T(2,128)}, f32[4,2,512]{2,1,0:T(2,128)}) custom-call(s32[4]{0:T(128)} %pad_add_fusion.1.info_ref, bf16[512,2048]{1,0:T(8,128)(2,1)} %collective-permute-done.4.refs_0_.refs_1_.refs_3_, bf16[512,2048]{1,0:T(8,128)(2,1)} %collective-permute-done.5.refs_1_.refs_4_, ...), custom_call_target="tpu_custom_call" | custom-call | flops 8589934592 | bytes 8388608 | tf_op jit(solution)/shard_map/attend_forward/pallas_call | solution.py:163
  220.1 13.6 %attend_forward.3 = (bf16[512,512]{1,0:T(8,128)(2,1)}, f32[4,2,512]{2,1,0:T(2,128)}) custom-call(s32[4]{0:T(128)} %pad_add_fusion.1.info_ref, bf16[512,512]{1,0:T(8,128)(2,1)} %get-tuple-element.87.refs_0_.refs_8_.refs_9_, bf16[512,512]{1,0:T(8,128)(2,1)} %get-tuple-element.92.refs_1_.refs_4_.refs_12_.refs_13_, ...), custom_call_target="tpu_custom_call" | custom-call | flops 4294967296 | bytes 8388608 | tf_op jit(solution)/shard_map/attend_forward/pallas_call | solution.py:163
  236.8 13.4 %collective-permute-start.16 = (bf16[256,2048]{1,0:T(8,128)(2,1)}, bf16[256,2048]{1,0:T(8,128)(2,1)}, u32[]{:S(2)}, u32[]{:S(2)}) collective-permute-start(bf16[256,2048]{1,0:T(8,128)(2,1)} %get-tuple-element.109), channel_id=1, source_target_pairs={{0,2},{1,3},{2,0},{3,1},{4,6},{5,7},{6,4},{7,5},{8,10},{9,11},{10,... | collective-permute-start | bytes 3145736 | tf_op jit(solution)/shard_map/ppermute | solution.py:989
  250.2 11.4 %collective-permute-start.17 = (bf16[256,2048]{1,0:T(8,128)(2,1)}, bf16[256,2048]{1,0:T(8,128)(2,1)}, u32[]{:S(2)}, u32[]{:S(2)}) collective-permute-start(bf16[256,2048]{1,0:T(8,128)(2,1)} %get-tuple-element.110), channel_id=1, source_target_pairs={{0,1},{1,0},{2,3},{3,2},{4,5},{5,4},{6,7},{7,6},{8,9},{9,8},{10,11... | collective-permute-start | bytes 3145736 | tf_op jit(solution)/shard_map/ppermute | solution.py:989
  268.1 8.0 settle.1
  276.3 13.1 %collective-permute-done.16.refs_0_ = bf16[256,2048]{1,0:T(8,128)(2,1)} collective-permute-done((bf16[256,2048]{1,0:T(8,128)(2,1)}, bf16[256,2048]{1,0:T(8,128)(2,1)}, u32[]{:S(2)}, u32[]{:S(2)}) %collective-permute-start.16) | collective-permute-done | bytes 1048608 | tf_op jit(solution)/shard_map/ppermute | solution.py:989
  292.4 25.8 %feed.4 = (bf16[2048,1408]{1,0:T(8,128)(2,1)}, bf16[2,2048,1408]{2,1,0:T(8,128)(2,1)}, f32[512,2048]{1,0:T(8,128)}) custom-call(bf16[512,2048]{1,0:T(8,128)(2,1)} %get-tuple-element.105.refs_0_.refs_4_, bf16[512,2048]{1,0:T(8,128)(2,1)} %shrink.1.refs_1_.refs_11_.refs_2_, bf16[2,2048,1408]{2,1,0:T(8,128)(2,1)} %all-gather.9.cloned.1.call-done.refs_2_.refs_3_, ...), custom_call_target="tpu_custom_call" | custom-call | flops 14763950080 | bytes 17301504 | tf_op jit(solution)/shard_map/feed/pallas_call | solution.py:457
  330.8 24.8 %feed.5 = (bf16[2048,1408]{1,0:T(8,128)(2,1)}, bf16[2,2048,1408]{2,1,0:T(8,128)(2,1)}, bf16[512,2048]{1,0:T(8,128)(2,1)}) custom-call(bf16[512,2048]{1,0:T(8,128)(2,1)} %collective-permute-done.12.refs_1_.refs_0_.refs_5_, bf16[512,2048]{1,0:T(8,128)(2,1)} %collective-permute-done.4.refs_0_.refs_1_.refs_3_, ...), custom_call_target="tpu_custom_call", output_to_operand_aliasing={{0}: (4, {}), {1}: (5, {})} | custom-call | flops 14763950080 | bytes 17301504 | tf_op jit(solution)/shard_map/feed/pallas_call | solution.py:457
  356.9 24.9 %feed.6 = (bf16[2048,1408]{1,0:T(8,128)(2,1)}, bf16[2,2048,1408]{2,1,0:T(8,128)(2,1)}, bf16[512,2048]{1,0:T(8,128)(2,1)}) custom-call(bf16[256,2048]{1,0:T(8,128)(2,1)} %copy-done.61, bf16[256,2048]{1,0:T(8,128)(2,1)} %copy-done.62, bf16[512,2048]{1,0:T(8,128)(2,1)} %join.3.refs_2_.refs_5_, ...), custom_call_target="tpu_custom_call", output_to_operand_aliasing={{0}: (5, {}), {1}: (6, {})} | custom-call | flops 14763950080 | bytes 17301504 | tf_op jit(solution)/shard_map/feed/pallas_call | solution.py:457
  385.7 24.6 %feed.7 = (bf16[2048,1408]{1,0:T(8,128)(2,1)}, bf16[2,2048,1408]{2,1,0:T(8,128)(2,1)}, bf16[512,2048]{1,0:T(8,128)(2,1)}) custom-call(bf16[512,2048]{1,0:T(8,128)(2,1)} %collective-permute-done.13.refs_2_.refs_0_.refs_6_, bf16[512,2048]{1,0:T(8,128)(2,1)} %collective-permute-done.5.refs_1_.refs_4_, ...), custom_call_target="tpu_custom_call", output_to_operand_aliasing={{0}: (4, {}), {1}: (5, {})} | custom-call | flops 14763950080 | bytes 17301504 | tf_op jit(solution)/shard_map/feed/pallas_call | solution.py:457
  414.8 34.0 %wide_grad.3.refs_0_ = bf16[2,2048,1408]{2,1,0:T(8,128)(2,1)} custom-call(bf16[256,2048]{1,0:T(8,128)(2,1)} %copy-done.36, bf16[256,2048]{1,0:T(8,128)(2,1)} %copy-done.37, bf16[256,2048]{1,0:T(8,128)(2,1)} %add_convert_fusion.5.refs_2_, bf16[256,2048]{1,0:T(8,128)(2,1)} %add_convert_fusion.4.refs_3_, bf16[512,2048]{1,0:T(8,128)(2,1)} %get-tuple-element.105.refs_0_.refs_4_, ...), custom_call_target="tpu_custom_call" | custom-call | flops 23622320128 | bytes 31457280 | tf_op jit(solution)/shard_map/wide_grad/pallas_call | solution.py:506
  456.6 20.6 %down_project.1 = (bf16[512,2048]{1,0:T(8,128)(2,1)}, bf16[512,2048]{1,0:T(8,128)(2,1)}, bf16[512,2048]{1,0:T(8,128)(2,1)}, bf16[512,2048]{1,0:T(8,128)(2,1)}) custom-call(bf16[2,2048,1408]{2,1,0:T(8,128)(2,1)} %wide_grad.3.refs_0_, bf16[2048,1408]{1,0:T(8,128)(2,1)} %get-tuple-element.120.refs_1_, ...), custom_call_target="tpu_custom_call" | custom-call | flops 11811160064 | bytes 19922944 | tf_op jit(solution)/shard_map/down_project/pallas_call | solution.py:924
  477.2 11.7 %collective-permute-done.21.refs_7_ = bf16[256,2048]{1,0:T(8,128)(2,1)S(1)} collective-permute-done((bf16[256,2048]{1,0:T(8,128)(2,1)S(1)}, bf16[256,2048]{1,0:T(8,128)(2,1)S(1)}, u32[]{:S(2)}, u32[]{:S(2)}) %collective-permute-start.21) | collective-permute-done | bytes 1048608 | tf_op jit(solution)/shard_map/ppermute | solution.py:989
  489.8 10.5 %unsettle.2 = (f32[512,2048]{1,0:T(8,128)}, bf16[512,2048]{1,0:T(8,128)(2,1)}, f32[1,2048]{1,0:T(1,128)}, f32[1,2048]{1,0:T(1,128)}) custom-call(bf16[2,2048,1408]{2,1,0:T(8,128)(2,1)} %wide_grad.3.refs_0_, bf16[512,2048]{1,0:T(8,128)(2,1)} %get-tuple-element.121.refs_1_.refs_3_, bf16[512,2048]{1,0:T(8,128)(2,1)} %get-tuple-element.122.refs_2_.refs_6_, ...), custom_call_target="tpu_custom_call" | custom-call | flops 20971520 | bytes 20971520 | tf_op jit(solution)/shard_map/unsettle/pallas_call | solution.py:762
  501.4 19.4 %tall_grad.2.refs_0_ = bf16[1408,2048]{1,0:T(8,128)(2,1)} custom-call(bf16[512,2048]{1,0:T(8,128)(2,1)} %get-tuple-element.127.refs_0_.refs_5_, bf16[2048,1408]{1,0:T(8,128)(2,1)} %get-tuple-element.120.refs_1_, bf16[512,2048]{1,0:T(8,128)(2,1)} %shrink.1.refs_1_.refs_11_.refs_2_, bf16[512,2048]{1,0:T(8,128)(2,1)} %collective-permute-done.4.refs_0_.refs_1_.refs_3_, ...), custom_call_target="tpu_custom_call" | custom-call | flops 11811160064 | bytes 19922944 | tf_op jit(solution)/shard_map/tall_grad/pallas_call | solution.py:547
  520.8 17.1 %collective-permute-done.24.refs_1_.refs_0_.refs_6_ = bf16[512,2048]{1,0:T(8,128)(2,1)} collective-permute-done((bf16[512,2048]{1,0:T(8,128)(2,1)}, bf16[512,2048]{1,0:T(8,128)(2,1)}, u32[]{:S(2)}, u32[]{:S(2)}) %collective-permute-start.24) | collective-permute-done | bytes 2097184 | tf_op jit(solution)/shard_map/ppermute | solution.py:989
  545.0 18.8 %collective-permute-done.26.refs_2_.refs_8_ = bf16[256,2048]{1,0:T(8,128)(2,1)S(1)} collective-permute-done((bf16[256,2048]{1,0:T(8,128)(2,1)}, bf16[256,2048]{1,0:T(8,128)(2,1)S(1)}, u32[]{:S(2)}, u32[]{:S(2)}) %collective-permute-start.26) | collective-permute-done | bytes 1048608 | tf_op jit(solution)/shard_map/ppermute | solution.py:989
  586.5 49.0 %attend_backward.2 = (bf16[3,2048,512]{2,1,0:T(8,128)(2,1)}, f32[3,256]{1,0:T(4,128)}) custom-call(s32[4]{0:T(128)} %pad_add_fusion.1.info_ref, bf16[2,256,1408]{2,1,0:T(8,128)(2,1)} %reduce-scatter.6.cloned.1.call-done.refs_0_, bf16[256,2048]{1,0:T(8,128)(2,1)} %collective-permute-done.28.refs_1_, bf16[256,2048]{1,0:T(8,128)(2,1)} %collective-permute-done.29.refs_2_, ...), custom_call_target="tpu_custom_call" | custom-call | flops 21474836480 | bytes 8388608 | tf_op jit(solution)/shard_map/attend_backward/pallas_call | solution.py:298
  635.5 12.6 %wide_grad.4.refs_0_.refs_4_ = bf16[3,2048,256]{2,1,0:T(8,128)(2,1)} custom-call(bf16[512,2048]{1,0:T(8,128)(2,1)} %fusion.5.x_ref.refs_0_.refs_5_, bf16[512,2048]{1,0:T(8,128)(2,1)} %collective-permute-done.x_ref.refs_0_.refs_1_.refs_6_, bf16[512,2048]{1,0:T(8,128)(2,1)} %copy-done.6, bf16[512,2048]{1,0:T(8,128)(2,1)} %join.2.x_ref.refs_2_.refs_3_.refs_8_, ...), custom_call_target="tpu_custom_call" | custom-call | flops 6442450944 | bytes 14680064 | tf_op jit(solution)/shard_map/wide_grad/pallas_call | solution.py:506
  648.9 11.2 %tall_grad.3.refs_1_ = bf16[512,2048]{1,0:T(8,128)(2,1)} custom-call(bf16[3,2048,256]{2,1,0:T(8,128)(2,1)} %wide_grad.4.refs_0_.refs_4_, bf16[512,512]{1,0:T(8,128)(2,1)} %get-tuple-element.100.refs_20_.refs_1_.refs_21_, bf16[512,512]{1,0:T(8,128)(2,1)} %get-tuple-element.101.refs_21_.refs_2_.refs_22_, ...), custom_call_target="tpu_custom_call" | custom-call | flops 4294967296 | bytes 12582912 | tf_op jit(solution)/shard_map/tall_grad/pallas_call | solution.py:547
  668.0 49.2 %attend_backward.3 = (bf16[3,2048,512]{2,1,0:T(8,128)(2,1)}, f32[3,256]{1,0:T(4,128)}) custom-call(s32[4]{0:T(128)} %pad_add_fusion.1.info_ref, bf16[3,2048,512]{2,1,0:T(8,128)(2,1)} %get-tuple-element.136.refs_4_.refs_0_, bf16[512,2048]{1,0:T(8,128)(2,1)} %tall_grad.3.refs_1_, bf16[256,2048]{1,0:T(8,128)(2,1)} %copy-done.28, ...), custom_call_target="tpu_custom_call", output_to_operand_aliasing={{0}: (1, {})} | custom-call | flops 21474836480 | bytes 8388608 | tf_op jit(solution)/shard_map/attend_backward/pallas_call | solution.py:298
  722.5 12.6 %wide_grad.5.refs_0_.refs_5_ = bf16[3,2048,256]{2,1,0:T(8,128)(2,1)} custom-call(bf16[3,256,256]{2,1,0:T(8,128)(2,1)} %reduce-scatter.8.cloned.1.call-done.refs_0_, bf16[256,2048]{1,0:T(8,128)(2,1)} %copy-done.23, bf16[256,2048]{1,0:T(8,128)(2,1)} %copy-done.24, bf16[256,2048]{1,0:T(8,128)(2,1)} %collective-permute-done.32.refs_3_.refs_6_, ...), custom_call_target="tpu_custom_call" | custom-call | flops 6442450944 | bytes 14680064 | tf_op jit(solution)/shard_map/wide_grad/pallas_call | solution.py:506
  735.1 53.8 %reduce-scatter.14.cloned.1.call-done = bf16[1408,256]{1,0:T(8,128)(2,1)} async-done(((bf16[1408,2048]{1,0:T(8,128)(2,1)}), bf16[1408,256]{1,0:T(8,128)(2,1)}) %reduce-scatter.14.cloned.1.call-update) | async-done | bytes 720912 | tf_op jit(solution)/shard_map/reduce_scatter | solution.py:1060
  793.3 19.3 %unproject.1 = (f32[512,2048]{1,0:T(8,128)}, bf16[512,2048]{1,0:T(8,128)(2,1)}, bf16[512,2048]{1,0:T(8,128)(2,1)}, bf16[512,2048]{1,0:T(8,128)(2,1)}) custom-call(bf16[3,2048,256]{2,1,0:T(8,128)(2,1)} %wide_grad.5.refs_0_.refs_5_, bf16[3,2048,512]{2,1,0:T(8,128)(2,1)} %get-tuple-element.139.refs_9_.refs_1_.refs_2_.refs_3_.refs_4_, ...), custom_call_target="tpu_custom_call" | custom-call | flops 12884901888 | bytes 29360128 | tf_op jit(solution)/shard_map/unproject/pallas_call | solution.py:800
  827.3 15.0 %collective-permute-done.37 = bf16[256,2048]{1,0:T(8,128)(2,1)} collective-permute-done((bf16[256,2048]{1,0:T(8,128)(2,1)}, bf16[256,2048]{1,0:T(8,128)(2,1)}, u32[]{:S(2)}, u32[]{:S(2)}) %collective-permute-start.37) | collective-permute-done | bytes 1048608 | tf_op jit(solution)/shard_map/ppermute | solution.py:989
  852.9 8.8 first_line.1
  875.3 9.6 %collective-permute-done.38.refs_4_.refs_2_ = bf16[256,2048]{1,0:T(8,128)(2,1)} collective-permute-done((bf16[256,2048]{1,0:T(8,128)(2,1)}, bf16[256,2048]{1,0:T(8,128)(2,1)}, u32[]{:S(2)}, u32[]{:S(2)}) %collective-permute-start.38) | collective-permute-done | bytes 1048608 | tf_op jit(solution)/shard_map/ppermute | solution.py:989
  904.7 10.1 %unsettle.3 = (f32[512,2048]{1,0:T(8,128)}, bf16[512,2048]{1,0:T(8,128)(2,1)}, f32[1,2048]{1,0:T(1,128)}, f32[1,2048]{1,0:T(1,128)}) custom-call(bf16[3,256,256]{2,1,0:T(8,128)(2,1)} %reduce-scatter.10.cloned.1.call-done.refs_0_, f32[512,2048]{1,0:T(8,128)} %get-tuple-element.143.refs_1_, bf16[256,2048]{1,0:T(8,128)(2,1)} %copy-done.10, ...), custom_call_target="tpu_custom_call" | custom-call | flops 20971520 | bytes 20971520 | tf_op jit(solution)/shard_map/unsettle/pallas_call | solution.py:762
  (310 shorter events, 236.5 us)
Async XLA Ops:
  7.2 71.2 %all-gather.5.cloned.1.call-start = ((), (), s32[]{:S(2)}) async-start(), calls=%async_computation.5 | async-start | bytes 7077888 | tf_op jit(solution)/shard_map/all_gather | solution.py:1098
  9.8 148.7 %all-gather.7.cloned.1.call-start = ((), (), s32[]{:S(2)}) async-start(), calls=%async_computation.6 | async-start | bytes 2359296 | tf_op jit(solution)/shard_map/all_gather | solution.py:1098
  10.6 281.7 %all-gather.11.cloned.1.call-start = ((), (), s32[]{:S(2)}) async-start(), calls=%async_computation.8 | async-start | bytes 6488064 | tf_op jit(solution)/shard_map/all_gather | solution.py:1098
  11.7 280.7 %all-gather.9.cloned.1.call-start = ((), (), s32[]{:S(2)}) async-start(), calls=%async_computation.7 | async-start | bytes 12976128 | tf_op jit(solution)/shard_map/all_gather | solution.py:1098
  15.0 571.5 %reduce-scatter.6.cloned.1.call-start = ((), (), s32[]{:S(2)}) async-start(), calls=%async_computation.9 | async-start | bytes 12976128 | tf_op jit(solution)/shard_map/reduce_scatter | solution.py:1060
  19.5 48.8 %collective-permute-start.1 = (bf16[512,2048]{1,0:T(8,128)(2,1)}, bf16[512,2048]{1,0:T(8,128)(2,1)S(1)}, u32[]{:S(2)}, u32[]{:S(2)}) collective-permute-start(bf16[512,2048]{1,0:T(8,128)(2,1)} %fusion.5.x_ref.refs_0_.refs_5_), channel_id=1, source_target_pairs={{0,2},{1,3},{2,0},{3,1},{4,6},{5,7},{6,4},{7,5},{8,10},{9,11},{10,... | collective-permute-start | bytes 6291464 | tf_op jit(solution)/shard_map/ppermute | solution.py:989
  22.4 47.4 %collective-permute-start = (bf16[512,2048]{1,0:T(8,128)(2,1)}, bf16[512,2048]{1,0:T(8,128)(2,1)}, u32[]{:S(2)}, u32[]{:S(2)}) collective-permute-start(bf16[512,2048]{1,0:T(8,128)(2,1)} %fusion.5.x_ref.refs_0_.refs_5_), channel_id=1, source_target_pairs={{0,1},{1,0},{2,3},{3,2},{4,5},{5,4},{6,7},{7,6},{8,9},{9,8},{10,11... | collective-permute-start | bytes 6291464 | tf_op jit(solution)/shard_map/ppermute | solution.py:989
  109.9 52.0 %collective-permute-start.4 = (bf16[512,2048]{1,0:T(8,128)(2,1)}, bf16[512,2048]{1,0:T(8,128)(2,1)}, u32[]{:S(2)}, u32[]{:S(2)}) collective-permute-start(bf16[512,2048]{1,0:T(8,128)(2,1)} %shrink.1.refs_1_.refs_11_.refs_2_), channel_id=1, source_target_pairs={{0,1},{1,0},{2,3},{3,2},{4,5},{5,4},{6,7},{7,6},{8,9},{9,8},{10,11... | collective-permute-start | bytes 6291464 | tf_op jit(solution)/shard_map/ppermute | solution.py:989
  110.8 51.1 %collective-permute-start.5 = (bf16[512,2048]{1,0:T(8,128)(2,1)}, bf16[512,2048]{1,0:T(8,128)(2,1)}, u32[]{:S(2)}, u32[]{:S(2)}) collective-permute-start(bf16[512,2048]{1,0:T(8,128)(2,1)} %shrink.1.refs_1_.refs_11_.refs_2_), channel_id=1, source_target_pairs={{0,2},{1,3},{2,0},{3,1},{4,6},{5,7},{6,4},{7,5},{8,10},{9,11},{10,... | collective-permute-start | bytes 6291464 | tf_op jit(solution)/shard_map/ppermute | solution.py:989
  161.7 43.8 %collective-permute-start.9 = (bf16[256,2048]{1,0:T(8,128)(2,1)S(1)}, bf16[256,2048]{1,0:T(8,128)(2,1)S(1)}, u32[]{:S(2)}, u32[]{:S(2)}) collective-permute-start(bf16[256,2048]{1,0:T(8,128)(2,1)S(1)} %get-tuple-element.174), channel_id=1, source_target_pairs={{0,2},{1,3},{2,0},{3,1},{4,6},{5,7},{6,4},{7,5},{8,10},{9,11},{10,... | collective-permute-start | bytes 3145736 | tf_op jit(solution)/shard_map/ppermute | solution.py:989
  161.8 54.9 %collective-permute-start.7 = (bf16[256,2048]{1,0:T(8,128)(2,1)S(1)}, bf16[256,2048]{1,0:T(8,128)(2,1)S(1)}, u32[]{:S(2)}, u32[]{:S(2)}) collective-permute-start(bf16[256,2048]{1,0:T(8,128)(2,1)S(1)} %get-tuple-element.175), channel_id=1, source_target_pairs={{0,1},{1,0},{2,3},{3,2},{4,5},{5,4},{6,7},{7,6},{8,9},{9,8},{10,11... | collective-permute-start | bytes 3145736 | tf_op jit(solution)/shard_map/ppermute | solution.py:989
  206.8 43.4 %collective-permute-start.10 = (bf16[256,2048]{1,0:T(8,128)(2,1)}, bf16[256,2048]{1,0:T(8,128)(2,1)S(1)}, u32[]{:S(2)}, u32[]{:S(2)}) collective-permute-start(bf16[256,2048]{1,0:T(8,128)(2,1)} %fusion.7), channel_id=1, source_target_pairs={{0,1},{1,0},{2,3},{3,2},{4,5},{5,4},{6,7},{7,6},{8,9},{9,8},{10,11... | collective-permute-start | bytes 3145736 | tf_op jit(solution)/shard_map/ppermute | solution.py:989
  218.0 46.9 %collective-permute-start.8 = (bf16[256,2048]{1,0:T(8,128)(2,1)}, bf16[256,2048]{1,0:T(8,128)(2,1)S(1)}, u32[]{:S(2)}, u32[]{:S(2)}) collective-permute-start(bf16[256,2048]{1,0:T(8,128)(2,1)} %fusion.8), channel_id=1, source_target_pairs={{0,2},{1,3},{2,0},{3,1},{4,6},{5,7},{6,4},{7,5},{8,10},{9,11},{10,... | collective-permute-start | bytes 3145736 | tf_op jit(solution)/shard_map/ppermute | solution.py:989
  218.0 48.7 %collective-permute-start.11 = (bf16[256,2048]{1,0:T(8,128)(2,1)}, bf16[256,2048]{1,0:T(8,128)(2,1)S(1)}, u32[]{:S(2)}, u32[]{:S(2)}) collective-permute-start(bf16[256,2048]{1,0:T(8,128)(2,1)} %slice.139), channel_id=1, source_target_pairs={{0,2},{1,3},{2,0},{3,1},{4,6},{5,7},{6,4},{7,5},{8,10},{9,11},{10,... | collective-permute-start | bytes 3145736 | tf_op jit(solution)/shard_map/ppermute | solution.py:989
  220.0 46.8 %collective-permute-start.6 = (bf16[256,2048]{1,0:T(8,128)(2,1)S(1)}, bf16[256,2048]{1,0:T(8,128)(2,1)S(1)}, u32[]{:S(2)}, u32[]{:S(2)}) collective-permute-start(bf16[256,2048]{1,0:T(8,128)(2,1)S(1)} %slice.140), channel_id=1, source_target_pairs={{0,1},{1,0},{2,3},{3,2},{4,5},{5,4},{6,7},{7,6},{8,9},{9,8},{10,11... | collective-permute-start | bytes 3145736 | tf_op jit(solution)/shard_map/ppermute | solution.py:989
  236.8 52.6 %collective-permute-start.16 = (bf16[256,2048]{1,0:T(8,128)(2,1)}, bf16[256,2048]{1,0:T(8,128)(2,1)}, u32[]{:S(2)}, u32[]{:S(2)}) collective-permute-start(bf16[256,2048]{1,0:T(8,128)(2,1)} %get-tuple-element.109), channel_id=1, source_target_pairs={{0,2},{1,3},{2,0},{3,1},{4,6},{5,7},{6,4},{7,5},{8,10},{9,11},{10,... | collective-permute-start | bytes 3145736 | tf_op jit(solution)/shard_map/ppermute | solution.py:989
  250.2 39.2 %collective-permute-start.17 = (bf16[256,2048]{1,0:T(8,128)(2,1)}, bf16[256,2048]{1,0:T(8,128)(2,1)}, u32[]{:S(2)}, u32[]{:S(2)}) collective-permute-start(bf16[256,2048]{1,0:T(8,128)(2,1)} %get-tuple-element.110), channel_id=1, source_target_pairs={{0,1},{1,0},{2,3},{3,2},{4,5},{5,4},{6,7},{7,6},{8,9},{9,8},{10,11... | collective-permute-start | bytes 3145736 | tf_op jit(solution)/shard_map/ppermute | solution.py:989
  276.1 42.1 %collective-permute-start.12 = (bf16[512,2048]{1,0:T(8,128)(2,1)}, bf16[512,2048]{1,0:T(8,128)(2,1)}, u32[]{:S(2)}, u32[]{:S(2)}) collective-permute-start(bf16[512,2048]{1,0:T(8,128)(2,1)} %get-tuple-element.105.refs_0_.refs_4_), channel_id=1, source_target_pairs={{0,1},{1,0},{2,3},{3,2},{4,5},{5,4},{6,7},{7,6},{8,9},{9,8},{10,11... | collective-permute-start | bytes 6291464 | tf_op jit(solution)/shard_map/ppermute | solution.py:989
  276.2 49.7 %collective-permute-start.13 = (bf16[512,2048]{1,0:T(8,128)(2,1)}, bf16[512,2048]{1,0:T(8,128)(2,1)}, u32[]{:S(2)}, u32[]{:S(2)}) collective-permute-start(bf16[512,2048]{1,0:T(8,128)(2,1)} %get-tuple-element.105.refs_0_.refs_4_), channel_id=1, source_target_pairs={{0,2},{1,3},{2,0},{3,1},{4,6},{5,7},{6,4},{7,5},{8,10},{9,11},{10,... | collective-permute-start | bytes 6291464 | tf_op jit(solution)/shard_map/ppermute | solution.py:989
  448.9 273.6 %reduce-scatter.8.cloned.1.call-start = ((), (), s32[]{:S(2)}) async-start(), calls=%async_computation.10 | async-start | bytes 3538944 | tf_op jit(solution)/shard_map/reduce_scatter | solution.py:1060
  500.3 37.6 %collective-permute-start.24 = (bf16[512,2048]{1,0:T(8,128)(2,1)}, bf16[512,2048]{1,0:T(8,128)(2,1)}, u32[]{:S(2)}, u32[]{:S(2)}) collective-permute-start(bf16[512,2048]{1,0:T(8,128)(2,1)} %get-tuple-element.127.refs_0_.refs_5_), channel_id=1, source_target_pairs={{0,1},{1,0},{2,3},{3,2},{4,5},{5,4},{6,7},{7,6},{8,9},{9,8},{10,11... | collective-permute-start | bytes 6291464 | tf_op jit(solution)/shard_map/ppermute | solution.py:989
  500.3 37.7 %collective-permute-start.25 = (bf16[512,2048]{1,0:T(8,128)(2,1)}, bf16[512,2048]{1,0:T(8,128)(2,1)}, u32[]{:S(2)}, u32[]{:S(2)}) collective-permute-start(bf16[512,2048]{1,0:T(8,128)(2,1)} %get-tuple-element.127.refs_0_.refs_5_), channel_id=1, source_target_pairs={{0,2},{1,3},{2,0},{3,1},{4,6},{5,7},{6,4},{7,5},{8,10},{9,11},{10,... | collective-permute-start | bytes 6291464 | tf_op jit(solution)/shard_map/ppermute | solution.py:989
  648.1 140.8 %reduce-scatter.14.cloned.1.call-start = ((), (), s32[]{:S(2)}) async-start(), calls=%async_computation.13 | async-start | bytes 6488064 | tf_op jit(solution)/shard_map/reduce_scatter | solution.py:1060
  648.9 201.7 %reduce-scatter.12.cloned.1.call-start = ((), (), s32[]{:S(2)}) async-start(), calls=%async_computation.12 | async-start | bytes 2359296 | tf_op jit(solution)/shard_map/reduce_scatter | solution.py:1060
  660.1 209.9 %reduce-scatter.10.cloned.1.call-start = ((), (), s32[]{:S(2)}) async-start(), calls=%async_computation.11 | async-start | bytes 3538944 | tf_op jit(solution)/shard_map/reduce_scatter | solution.py:1060
  660.2 57.0 %collective-permute-start.30 = (bf16[256,2048]{1,0:T(8,128)(2,1)}, bf16[256,2048]{1,0:T(8,128)(2,1)S(1)}, u32[]{:S(2)}, u32[]{:S(2)}) collective-permute-start(bf16[256,2048]{1,0:T(8,128)(2,1)} %get-tuple-element.137), channel_id=1, source_target_pairs={{0,1},{1,0},{2,3},{3,2},{4,5},{5,4},{6,7},{7,6},{8,9},{9,8},{10,11... | collective-permute-start | bytes 3145736 | tf_op jit(solution)/shard_map/ppermute | solution.py:989
  661.0 56.2 %collective-permute-start.33 = (bf16[256,2048]{1,0:T(8,128)(2,1)}, bf16[256,2048]{1,0:T(8,128)(2,1)}, u32[]{:S(2)}, u32[]{:S(2)}) collective-permute-start(bf16[256,2048]{1,0:T(8,128)(2,1)} %get-tuple-element.138), channel_id=1, source_target_pairs={{0,2},{1,3},{2,0},{3,1},{4,6},{5,7},{6,4},{7,5},{8,10},{9,11},{10,... | collective-permute-start | bytes 3145736 | tf_op jit(solution)/shard_map/ppermute | solution.py:989
  664.2 53.0 %collective-permute-start.32 = (bf16[256,2048]{1,0:T(8,128)(2,1)S(1)}, bf16[256,2048]{1,0:T(8,128)(2,1)}, u32[]{:S(2)}, u32[]{:S(2)}) collective-permute-start(bf16[256,2048]{1,0:T(8,128)(2,1)S(1)} %add_convert_fusion.2.refs_2_), channel_id=1, source_target_pairs={{0,1},{1,0},{2,3},{3,2},{4,5},{5,4},{6,7},{7,6},{8,9},{9,8},{10,11... | collective-permute-start | bytes 3145736 | tf_op jit(solution)/shard_map/ppermute | solution.py:989
  666.6 50.7 %collective-permute-start.31 = (bf16[256,2048]{1,0:T(8,128)(2,1)S(1)}, bf16[256,2048]{1,0:T(8,128)(2,1)S(1)}, u32[]{:S(2)}, u32[]{:S(2)}) collective-permute-start(bf16[256,2048]{1,0:T(8,128)(2,1)S(1)} %add_convert_fusion.3.refs_3_), channel_id=1, source_target_pairs={{0,2},{1,3},{2,0},{3,1},{4,6},{5,7},{6,4},{7,5},{8,10},{9,11},{10,... | collective-permute-start | bytes 3145736 | tf_op jit(solution)/shard_map/ppermute | solution.py:989
  824.9 50.4 %collective-permute-start.34 = (bf16[256,2048]{1,0:T(8,128)(2,1)}, bf16[256,2048]{1,0:T(8,128)(2,1)S(1)}, u32[]{:S(2)}, u32[]{:S(2)}) collective-permute-start(bf16[256,2048]{1,0:T(8,128)(2,1)} %slice.103), channel_id=1, source_target_pairs={{0,1},{1,0},{2,3},{3,2},{4,5},{5,4},{6,7},{7,6},{8,9},{9,8},{10,11... | collective-permute-start | bytes 3145736 | tf_op jit(solution)/shard_map/ppermute | solution.py:989
  826.8 48.5 %collective-permute-start.39 = (bf16[256,2048]{1,0:T(8,128)(2,1)}, bf16[256,2048]{1,0:T(8,128)(2,1)}, u32[]{:S(2)}, u32[]{:S(2)}) collective-permute-start(bf16[256,2048]{1,0:T(8,128)(2,1)} %slice.108), channel_id=1, source_target_pairs={{0,2},{1,3},{2,0},{3,1},{4,6},{5,7},{6,4},{7,5},{8,10},{9,11},{10,... | collective-permute-start | bytes 3145736 | tf_op jit(solution)/shard_map/ppermute | solution.py:989
  844.9 40.0 %collective-permute-start.38 = (bf16[256,2048]{1,0:T(8,128)(2,1)}, bf16[256,2048]{1,0:T(8,128)(2,1)}, u32[]{:S(2)}, u32[]{:S(2)}) collective-permute-start(bf16[256,2048]{1,0:T(8,128)(2,1)} %add_convert_fusion), channel_id=1, source_target_pairs={{0,1},{1,0},{2,3},{3,2},{4,5},{5,4},{6,7},{7,6},{8,9},{9,8},{10,11... | collective-permute-start | bytes 3145736 | tf_op jit(solution)/shard_map/ppermute | solution.py:989
  (85 other events, 1028.3 us)
Sparse Core Ops, SparseCore 0:
  10.2 67.4 all-gather.4
  79.8 29.5 all-gather.6
  111.0 59.8 all-gather.10
  173.0 106.2 all-gather.8
  449.0 125.4 reduce-scatter.5
  648.2 74.2 reduce-scatter.7
  724.8 64.0 reduce-scatter.13
  791.2 34.1 reduce-scatter.11
  827.7 39.0 reduce-scatter.9

commit v2 on v1

--- a/solution.py
+++ b/solution.py
@@ -1207,7 +1207,7 @@
     layer_out = finish(layer_own, layer_rest, hidden, parts[1:])
     second_grad = scatter_weight(second_partial)
     qkv_grad = wide(jnp.concatenate([first_grad, second_grad], axis=2))
-    out_grad, gate_up_grad, down_grad = wide(out_grad), wide(gate_up_grad), wide(down_grad)
+    gate_up_grad = wide(gate_up_grad)
     input_grad = unsettle(
         *settled, hidden_in, grad_hidden, norm_gain[:1], [second_grad]
     )[0]
@@ -1225,16 +1225,16 @@
     qkv_first_new, qkv_second_new, qkv_new = adam_update(
         qkv_weight, qkv_grad, qkv_first, qkv_second, RATE_QKV, WEIGHT_DECAY
     )
-    out_first_new, out_second_new, out_new = adam_update(
-        out_weight, out_grad, out_first, out_second, RATE_OUT, WEIGHT_DECAY
-    )
     gate_up_first_new, gate_up_second_new, gate_up_new = adam_update(
         gate_up_weight, gate_up_grad, gate_up_first, gate_up_second, RATE_GATE_UP, WEIGHT_DECAY
     )
-    down_first_new, down_second_new, down_new = adam_update(
-        down_weight, down_grad, down_first, down_second, RATE_DOWN, WEIGHT_DECAY
-    )
-    settled_all = list(settled[1]) + [layer_out, down_new, gate_up_new, out_new, qkv_new]
+    settled_all = list(settled[1]) + [layer_out, gate_up_new]
+    down_grad, down_first_new, down_second_new, down_new = adam(
+        down_weight, down_grad, down_first, down_second, RATE_DOWN, settled[1]
+    )
+    out_grad, out_first_new, out_second_new, out_new = adam(
+        out_weight, out_grad, out_first, out_second, RATE_OUT, settled[1]
+    )
     small_grad = sum_along(sum_along(hold(small_grad, settled_all), "tensor"), "dp")
     small_first_new, small_second_new, small_new = adam_update(
         small_weight, small_grad, small_first, small_second, RATE_SMALL, 0.0

time: 932 us -> 877 us (0.941)
  waiting for transfers between devices: 204 us -> 121 us
  Pallas kernels: 522 us -> 548 us
    reduce_scatter x5, waiting for transfers between devices: 59 us -> 0.05 us  [scatter_weight(): return lax.psum_scatter(partial, 'dp', scatter_dimension=1, tiled=True)]
    ppermute x45, waiting for transfers between devices: 144 us -> 120 us  [swap(): return lax.ppermute(values, axis, [(at, at ^ bits) for at in range(size)])]
    pallas_call x0 -> x2, Pallas kernels: none -> 9.95 us  [adam(): pl.pallas_call(functools.partial(adam_kernel, rate, WEIGHT_DECAY, len(aft...]
  transfers between devices with their start and end apart: 54 -> 54, of which waited for: 19 -> 16; matrix products, arithmetic and copies ran while one was open for 10% -> 9% of each run, Pallas kernels for 43% -> 47%
where the time goes in v2:
time: 877 us; the launch traced here: 867 us
  Pallas kernels  548 us (62%)
  waiting for transfers between devices  121 us (14%)
  starting transfers between devices  83.7 us (10%)
  other arithmetic  50.7 us (6%)
  local copies, waits for them, and re-layouts  25.1 us (3%)
  matrix products  22.4 us (3%)
  between operations  17 us (2%)
    ppermute x45, waiting for transfers between devices, swap(): return lax.ppermute(values, axis, [(at, at ^ bits) for at in range(size)])  120 us
    pallas_call x2, Pallas kernels, attend_backward(): pl.pallas_call(functools.partial(attend_backward_kernel, count, len(grad_...  106 us
    pallas_call x4, Pallas kernels, feed(): pl.pallas_call(functools.partial(feed_kernel, len(held), split, cut, len(...  100 us
    pallas_call x3, Pallas kernels, attend_forward(): pl.pallas_call(functools.partial(attend_forward_kernel, tuple(chunks), co...  99.7 us
    ppermute x45, starting transfers between devices, swap(): return lax.ppermute(values, axis, [(at, at ^ bits) for at in range(size)])  83.3 us
    pallas_call x3, Pallas kernels, wide_grad(): pl.pallas_call(functools.partial(wide_grad_kernel, len(lefts), len(after)...  59.1 us
    pallas_call x4, Pallas kernels, project(): pl.pallas_call(project_kernel, grid=(rows // block,), in_specs=[pl.BlockS...  31.1 us
    pallas_call x2, Pallas kernels, tall_grad(): pl.pallas_call(functools.partial(tall_grad_kernel, held, count, len(after...  30.8 us
  transfers between devices with their start and end apart: 54, of which 16 were waited for; matrix products, arithmetic and copies ran while one was open for 9% of the time, Pallas kernels for 47%

profile of v2, /device:TPU:0, one launch (start us, length us, event | category | flops | bytes accessed | tf_op | source)
XLA Modules:
  0.0 866.9 jit_solution(17977092207292632418)
XLA Ops:
  35.0 33.2 %collective-permute-done.1.x_ref.refs_1_.refs_2_.refs_7_ = bf16[512,2048]{1,0:T(8,128)(2,1)S(1)} collective-permute-done((bf16[512,2048]{1,0:T(8,128)(2,1)}, bf16[512,2048]{1,0:T(8,128)(2,1)S(1)}, u32[]{:S(2)}, u32[]{:S(2)}) %collective-permute-start.1) | collective-permute-done | bytes 2097184 | tf_op jit(solution)/shard_map/ppermute | solution.py:989
  78.4 7.7 project.6
  86.1 7.8 project.5
  93.8 7.7 project.4
  114.2 7.9 project.7
  122.1 27.9 %attend_forward.5 = (bf16[512,512]{1,0:T(8,128)(2,1)}, f32[4,2,512]{2,1,0:T(2,128)}) custom-call(s32[4]{0:T(128)} %pad_add_fusion.1.info_ref, bf16[512,512]{1,0:T(8,128)(2,1)} %get-tuple-element.111.refs_0_.refs_11_.refs_12_, bf16[512,512]{1,0:T(8,128)(2,1)} %get-tuple-element.100.refs_1_.refs_4_.refs_12_.refs_13_, ...), custom_call_target="tpu_custom_call" | custom-call | flops 4294967296 | bytes 8388608 | tf_op jit(solution)/shard_map/attend_forward/pallas_call | solution.py:163
  153.3 9.0 %collective-permute-start.7 = (bf16[256,2048]{1,0:T(8,128)(2,1)S(1)}, bf16[256,2048]{1,0:T(8,128)(2,1)S(1)}, u32[]{:S(2)}, u32[]{:S(2)}) collective-permute-start(bf16[256,2048]{1,0:T(8,128)(2,1)S(1)} %get-tuple-element.183), channel_id=1, source_target_pairs={{0,1},{1,0},{2,3},{3,2},{4,5},{5,4},{6,7},{7,6},{8,9},{9,8},{10,11... | collective-permute-start | bytes 3145736 | tf_op jit(solution)/shard_map/ppermute | solution.py:989
  162.3 58.2 %attend_forward.4 = (bf16[512,512]{1,0:T(8,128)(2,1)}, bf16[512,512]{1,0:T(8,128)(2,1)}, f32[4,2,512]{2,1,0:T(2,128)}, f32[4,2,512]{2,1,0:T(2,128)}) custom-call(s32[4]{0:T(128)} %pad_add_fusion.1.info_ref, bf16[512,2048]{1,0:T(8,128)(2,1)} %collective-permute-done.4.refs_0_.refs_1_.refs_3_, bf16[512,2048]{1,0:T(8,128)(2,1)} %collective-permute-done.5.refs_1_.refs_4_, ...), custom_call_target="tpu_custom_call" | custom-call | flops 8589934592 | bytes 8388608 | tf_op jit(solution)/shard_map/attend_forward/pallas_call | solution.py:163
  232.0 13.6 %attend_forward.3 = (bf16[512,512]{1,0:T(8,128)(2,1)}, f32[4,2,512]{2,1,0:T(2,128)}) custom-call(s32[4]{0:T(128)} %pad_add_fusion.1.info_ref, bf16[512,512]{1,0:T(8,128)(2,1)} %get-tuple-element.95.refs_0_.refs_8_.refs_9_, bf16[512,512]{1,0:T(8,128)(2,1)} %get-tuple-element.100.refs_1_.refs_4_.refs_12_.refs_13_, ...), custom_call_target="tpu_custom_call" | custom-call | flops 4294967296 | bytes 8388608 | tf_op jit(solution)/shard_map/attend_forward/pallas_call | solution.py:163
  248.7 22.9 %collective-permute-start.16 = (bf16[256,2048]{1,0:T(8,128)(2,1)}, bf16[256,2048]{1,0:T(8,128)(2,1)}, u32[]{:S(2)}, u32[]{:S(2)}) collective-permute-start(bf16[256,2048]{1,0:T(8,128)(2,1)} %get-tuple-element.117), channel_id=1, source_target_pairs={{0,2},{1,3},{2,0},{3,1},{4,6},{5,7},{6,4},{7,5},{8,10},{9,11},{10,... | collective-permute-start | bytes 3145736 | tf_op jit(solution)/shard_map/ppermute | solution.py:989
  277.0 8.0 settle.1
  287.5 10.8 %collective-permute-done.16.refs_0_ = bf16[256,2048]{1,0:T(8,128)(2,1)} collective-permute-done((bf16[256,2048]{1,0:T(8,128)(2,1)}, bf16[256,2048]{1,0:T(8,128)(2,1)}, u32[]{:S(2)}, u32[]{:S(2)}) %collective-permute-start.16) | collective-permute-done | bytes 1048608 | tf_op jit(solution)/shard_map/ppermute | solution.py:989
  301.3 25.8 %feed.4 = (bf16[2048,1408]{1,0:T(8,128)(2,1)}, bf16[2,2048,1408]{2,1,0:T(8,128)(2,1)}, f32[512,2048]{1,0:T(8,128)}) custom-call(bf16[512,2048]{1,0:T(8,128)(2,1)} %get-tuple-element.113.refs_0_.refs_4_, bf16[512,2048]{1,0:T(8,128)(2,1)} %shrink.1.refs_1_.refs_11_.refs_2_, bf16[2,2048,1408]{2,1,0:T(8,128)(2,1)} %all-gather.9.cloned.1.call-done.refs_2_.refs_3_, ...), custom_call_target="tpu_custom_call" | custom-call | flops 14763950080 | bytes 17301504 | tf_op jit(solution)/shard_map/feed/pallas_call | solution.py:457
  337.8 24.8 %feed.5 = (bf16[2048,1408]{1,0:T(8,128)(2,1)}, bf16[2,2048,1408]{2,1,0:T(8,128)(2,1)}, bf16[512,2048]{1,0:T(8,128)(2,1)}) custom-call(bf16[512,2048]{1,0:T(8,128)(2,1)} %collective-permute-done.12.refs_1_.refs_0_.refs_5_, bf16[512,2048]{1,0:T(8,128)(2,1)} %collective-permute-done.4.refs_0_.refs_1_.refs_3_, ...), custom_call_target="tpu_custom_call", output_to_operand_aliasing={{0}: (4, {}), {1}: (5, {})} | custom-call | flops 14763950080 | bytes 17301504 | tf_op jit(solution)/shard_map/feed/pallas_call | solution.py:457
  363.9 24.9 %feed.6 = (bf16[2048,1408]{1,0:T(8,128)(2,1)}, bf16[2,2048,1408]{2,1,0:T(8,128)(2,1)}, bf16[512,2048]{1,0:T(8,128)(2,1)}) custom-call(bf16[256,2048]{1,0:T(8,128)(2,1)} %copy-done.59, bf16[256,2048]{1,0:T(8,128)(2,1)} %copy-done.60, bf16[512,2048]{1,0:T(8,128)(2,1)} %join.3.refs_2_.refs_5_, ...), custom_call_target="tpu_custom_call", output_to_operand_aliasing={{0}: (5, {}), {1}: (6, {})} | custom-call | flops 14763950080 | bytes 17301504 | tf_op jit(solution)/shard_map/feed/pallas_call | solution.py:457
  392.6 24.6 %feed.7 = (bf16[2048,1408]{1,0:T(8,128)(2,1)}, bf16[2,2048,1408]{2,1,0:T(8,128)(2,1)}, bf16[512,2048]{1,0:T(8,128)(2,1)}) custom-call(bf16[512,2048]{1,0:T(8,128)(2,1)} %collective-permute-done.13.refs_2_.refs_0_.refs_6_, bf16[512,2048]{1,0:T(8,128)(2,1)} %collective-permute-done.5.refs_1_.refs_4_, ...), custom_call_target="tpu_custom_call", output_to_operand_aliasing={{0}: (4, {}), {1}: (5, {})} | custom-call | flops 14763950080 | bytes 17301504 | tf_op jit(solution)/shard_map/feed/pallas_call | solution.py:457
  421.7 34.0 %wide_grad.3.refs_0_ = bf16[2,2048,1408]{2,1,0:T(8,128)(2,1)} custom-call(bf16[256,2048]{1,0:T(8,128)(2,1)} %copy-done.35, bf16[256,2048]{1,0:T(8,128)(2,1)} %copy-done.36, bf16[256,2048]{1,0:T(8,128)(2,1)} %add_convert_fusion.5.refs_2_, bf16[256,2048]{1,0:T(8,128)(2,1)} %add_convert_fusion.4.refs_3_, bf16[512,2048]{1,0:T(8,128)(2,1)} %get-tuple-element.113.refs_0_.refs_4_, ...), custom_call_target="tpu_custom_call" | custom-call | flops 23622320128 | bytes 31457280 | tf_op jit(solution)/shard_map/wide_grad/pallas_call | solution.py:506
  463.4 20.6 %down_project.1 = (bf16[512,2048]{1,0:T(8,128)(2,1)}, bf16[512,2048]{1,0:T(8,128)(2,1)}, bf16[512,2048]{1,0:T(8,128)(2,1)}, bf16[512,2048]{1,0:T(8,128)(2,1)}) custom-call(bf16[2,2048,1408]{2,1,0:T(8,128)(2,1)} %wide_grad.3.refs_0_, bf16[2048,1408]{1,0:T(8,128)(2,1)} %get-tuple-element.128.refs_1_, ...), custom_call_target="tpu_custom_call" | custom-call | flops 11811160064 | bytes 19922944 | tf_op jit(solution)/shard_map/down_project/pallas_call | solution.py:924
  484.1 14.9 %collective-permute-done.21.refs_7_ = bf16[256,2048]{1,0:T(8,128)(2,1)S(1)} collective-permute-done((bf16[256,2048]{1,0:T(8,128)(2,1)S(1)}, bf16[256,2048]{1,0:T(8,128)(2,1)S(1)}, u32[]{:S(2)}, u32[]{:S(2)}) %collective-permute-start.21) | collective-permute-done | bytes 1048608 | tf_op jit(solution)/shard_map/ppermute | solution.py:989
  499.9 10.5 %unsettle.2 = (f32[512,2048]{1,0:T(8,128)}, bf16[512,2048]{1,0:T(8,128)(2,1)}, f32[1,2048]{1,0:T(1,128)}, f32[1,2048]{1,0:T(1,128)}) custom-call(bf16[2,2048,1408]{2,1,0:T(8,128)(2,1)} %wide_grad.3.refs_0_, bf16[512,2048]{1,0:T(8,128)(2,1)} %get-tuple-element.129.refs_1_.refs_3_, bf16[512,2048]{1,0:T(8,128)(2,1)} %get-tuple-element.130.refs_2_.refs_6_, ...), custom_call_target="tpu_custom_call" | custom-call | flops 20971520 | bytes 20971520 | tf_op jit(solution)/shard_map/unsettle/pallas_call | solution.py:762
  515.2 19.5 %tall_grad.2.refs_0_ = bf16[1408,2048]{1,0:T(8,128)(2,1)} custom-call(bf16[512,2048]{1,0:T(8,128)(2,1)} %get-tuple-element.135.refs_0_.refs_5_, bf16[2048,1408]{1,0:T(8,128)(2,1)} %get-tuple-element.128.refs_1_, bf16[512,2048]{1,0:T(8,128)(2,1)} %shrink.1.refs_1_.refs_11_.refs_2_, bf16[512,2048]{1,0:T(8,128)(2,1)} %collective-permute-done.4.refs_0_.refs_1_.refs_3_, ...), custom_call_target="tpu_custom_call" | custom-call | flops 11811160064 | bytes 19922944 | tf_op jit(solution)/shard_map/tall_grad/pallas_call | solution.py:547
  534.7 14.7 %collective-permute-done.24.refs_1_.refs_0_.refs_6_ = bf16[512,2048]{1,0:T(8,128)(2,1)} collective-permute-done((bf16[512,2048]{1,0:T(8,128)(2,1)}, bf16[512,2048]{1,0:T(8,128)(2,1)}, u32[]{:S(2)}, u32[]{:S(2)}) %collective-permute-start.24) | collective-permute-done | bytes 2097184 | tf_op jit(solution)/shard_map/ppermute | solution.py:989
  559.7 11.1 %collective-permute-done.26.refs_2_.refs_8_ = bf16[256,2048]{1,0:T(8,128)(2,1)S(1)} collective-permute-done((bf16[256,2048]{1,0:T(8,128)(2,1)}, bf16[256,2048]{1,0:T(8,128)(2,1)S(1)}, u32[]{:S(2)}, u32[]{:S(2)}) %collective-permute-start.26) | collective-permute-done | bytes 1048608 | tf_op jit(solution)/shard_map/ppermute | solution.py:989
  593.9 52.7 %attend_backward.2 = (bf16[3,2048,512]{2,1,0:T(8,128)(2,1)}, f32[3,256]{1,0:T(4,128)}) custom-call(s32[4]{0:T(128)} %pad_add_fusion.1.info_ref, bf16[2,256,1408]{2,1,0:T(8,128)(2,1)} %reduce-scatter.6.cloned.1.call-done.refs_0_, bf16[256,2048]{1,0:T(8,128)(2,1)} %collective-permute-done.28.refs_1_, bf16[256,2048]{1,0:T(8,128)(2,1)} %collective-permute-done.29.refs_2_, ...), custom_call_target="tpu_custom_call" | custom-call | flops 21474836480 | bytes 8388608 | tf_op jit(solution)/shard_map/attend_backward/pallas_call | solution.py:298
  646.6 12.6 %wide_grad.4.refs_0_.refs_4_ = bf16[3,2048,256]{2,1,0:T(8,128)(2,1)} custom-call(bf16[512,2048]{1,0:T(8,128)(2,1)} %fusion.5.x_ref.refs_0_.refs_5_, bf16[512,2048]{1,0:T(8,128)(2,1)} %collective-permute-done.x_ref.refs_0_.refs_1_.refs_6_, bf16[512,2048]{1,0:T(8,128)(2,1)} %copy-done.9, bf16[512,2048]{1,0:T(8,128)(2,1)} %join.2.x_ref.refs_2_.refs_3_.refs_8_, ...), custom_call_target="tpu_custom_call" | custom-call | flops 6442450944 | bytes 14680064 | tf_op jit(solution)/shard_map/wide_grad/pallas_call | solution.py:506
  659.2 11.2 %tall_grad.3.refs_1_ = bf16[512,2048]{1,0:T(8,128)(2,1)} custom-call(bf16[3,2048,256]{2,1,0:T(8,128)(2,1)} %wide_grad.4.refs_0_.refs_4_, bf16[512,512]{1,0:T(8,128)(2,1)} %get-tuple-element.108.refs_20_.refs_1_.refs_21_, bf16[512,512]{1,0:T(8,128)(2,1)} %get-tuple-element.109.refs_21_.refs_2_.refs_22_, ...), custom_call_target="tpu_custom_call" | custom-call | flops 4294967296 | bytes 12582912 | tf_op jit(solution)/shard_map/tall_grad/pallas_call | solution.py:547
  679.8 53.0 %attend_backward.3 = (bf16[3,2048,512]{2,1,0:T(8,128)(2,1)}, f32[3,256]{1,0:T(4,128)}) custom-call(s32[4]{0:T(128)} %pad_add_fusion.1.info_ref, bf16[3,2048,512]{2,1,0:T(8,128)(2,1)} %get-tuple-element.144.refs_4_.refs_0_, bf16[512,2048]{1,0:T(8,128)(2,1)} %tall_grad.3.refs_1_, bf16[256,2048]{1,0:T(8,128)(2,1)} %copy-done.27, ...), custom_call_target="tpu_custom_call", output_to_operand_aliasing={{0}: (1, {})} | custom-call | flops 21474836480 | bytes 8388608 | tf_op jit(solution)/shard_map/attend_backward/pallas_call | solution.py:298
  734.0 12.6 %wide_grad.5.refs_0_.refs_5_ = bf16[3,2048,256]{2,1,0:T(8,128)(2,1)} custom-call(bf16[3,256,256]{2,1,0:T(8,128)(2,1)} %reduce-scatter.8.cloned.1.call-done.refs_0_, bf16[256,2048]{1,0:T(8,128)(2,1)} %copy-done.22, bf16[256,2048]{1,0:T(8,128)(2,1)} %copy-done.23, bf16[256,2048]{1,0:T(8,128)(2,1)} %collective-permute-done.32.refs_3_.refs_6_, ...), custom_call_target="tpu_custom_call" | custom-call | flops 6442450944 | bytes 14680064 | tf_op jit(solution)/shard_map/wide_grad/pallas_call | solution.py:506
  746.6 19.2 %unproject.1 = (f32[512,2048]{1,0:T(8,128)}, bf16[512,2048]{1,0:T(8,128)(2,1)}, bf16[512,2048]{1,0:T(8,128)(2,1)}, bf16[512,2048]{1,0:T(8,128)(2,1)}) custom-call(bf16[3,2048,256]{2,1,0:T(8,128)(2,1)} %wide_grad.5.refs_0_.refs_5_, bf16[3,2048,512]{2,1,0:T(8,128)(2,1)} %get-tuple-element.147.refs_9_.refs_1_.refs_2_.refs_3_.refs_4_, ...), custom_call_target="tpu_custom_call" | custom-call | flops 12884901888 | bytes 29360128 | tf_op jit(solution)/shard_map/unproject/pallas_call | solution.py:800
  773.9 9.2 %collective-permute-done.37 = bf16[256,2048]{1,0:T(8,128)(2,1)S(1)} collective-permute-done((bf16[256,2048]{1,0:T(8,128)(2,1)S(1)}, bf16[256,2048]{1,0:T(8,128)(2,1)S(1)}, u32[]{:S(2)}, u32[]{:S(2)}) %collective-permute-start.37) | collective-permute-done | bytes 1048608 | tf_op jit(solution)/shard_map/ppermute | solution.py:989
  794.3 8.7 %first_line.1 = f32[2,2048]{1,0:T(2,128)} custom-call(bf16[512,2048]{1,0:T(8,128)(2,1)} %get-tuple-element.148.refs_0_, bf16[512,2048]{1,0:T(8,128)(2,1)} %get-tuple-element.149.refs_1_, bf16[512,2048]{1,0:T(8,128)(2,1)} %get-tuple-element.150.refs_2_, bf16[3,2048,512]{2,1,0:T(8,128)(2,1)} %all-gather.5.cloned.1.call-done.w_ref.refs_5_.refs_3_, ...), custom_call_target="tpu_custom_call" | custom-call | flops 12582912 | bytes 12582912 | tf_op jit(solution)/shard_map/first_line/pallas_call | solution.py:891
  850.1 10.1 %unsettle.3 = (f32[512,2048]{1,0:T(8,128)}, bf16[512,2048]{1,0:T(8,128)(2,1)}, f32[1,2048]{1,0:T(1,128)}, f32[1,2048]{1,0:T(1,128)}) custom-call(bf16[3,256,256]{2,1,0:T(8,128)(2,1)} %reduce-scatter.10.cloned.1.call-done.refs_0_, f32[512,2048]{1,0:T(8,128)} %get-tuple-element.151.refs_1_, bf16[256,2048]{1,0:T(8,128)(2,1)} %copy-done.4, ...), custom_call_target="tpu_custom_call" | custom-call | flops 20971520 | bytes 20971520 | tf_op jit(solution)/shard_map/unsettle/pallas_call | solution.py:762
  (306 shorter events, 220.8 us)
Async XLA Ops:
  7.2 71.2 %all-gather.5.cloned.1.call-start = ((), (), s32[]{:S(2)}) async-start(), calls=%async_computation.5 | async-start | bytes 7077888 | tf_op jit(solution)/shard_map/all_gather | solution.py:1098
  9.8 140.2 %all-gather.7.cloned.1.call-start = ((), (), s32[]{:S(2)}) async-start(), calls=%async_computation.6 | async-start | bytes 2359296 | tf_op jit(solution)/shard_map/all_gather | solution.py:1098
  10.6 290.7 %all-gather.11.cloned.1.call-start = ((), (), s32[]{:S(2)}) async-start(), calls=%async_computation.8 | async-start | bytes 6488064 | tf_op jit(solution)/shard_map/all_gather | solution.py:1098
  11.6 289.7 %all-gather.9.cloned.1.call-start = ((), (), s32[]{:S(2)}) async-start(), calls=%async_computation.7 | async-start | bytes 12976128 | tf_op jit(solution)/shard_map/all_gather | solution.py:1098
  14.9 578.9 %reduce-scatter.6.cloned.1.call-start = ((), (), s32[]{:S(2)}) async-start(), calls=%async_computation.9 | async-start | bytes 12976128 | tf_op jit(solution)/shard_map/reduce_scatter | solution.py:1060
  19.5 48.8 %collective-permute-start.1 = (bf16[512,2048]{1,0:T(8,128)(2,1)}, bf16[512,2048]{1,0:T(8,128)(2,1)S(1)}, u32[]{:S(2)}, u32[]{:S(2)}) collective-permute-start(bf16[512,2048]{1,0:T(8,128)(2,1)} %fusion.5.x_ref.refs_0_.refs_5_), channel_id=1, source_target_pairs={{0,2},{1,3},{2,0},{3,1},{4,6},{5,7},{6,4},{7,5},{8,10},{9,11},{10,... | collective-permute-start | bytes 6291464 | tf_op jit(solution)/shard_map/ppermute | solution.py:989
  22.4 47.4 %collective-permute-start = (bf16[512,2048]{1,0:T(8,128)(2,1)}, bf16[512,2048]{1,0:T(8,128)(2,1)}, u32[]{:S(2)}, u32[]{:S(2)}) collective-permute-start(bf16[512,2048]{1,0:T(8,128)(2,1)} %fusion.5.x_ref.refs_0_.refs_5_), channel_id=1, source_target_pairs={{0,1},{1,0},{2,3},{3,2},{4,5},{5,4},{6,7},{7,6},{8,9},{9,8},{10,11... | collective-permute-start | bytes 6291464 | tf_op jit(solution)/shard_map/ppermute | solution.py:989
  109.9 52.4 %collective-permute-start.4 = (bf16[512,2048]{1,0:T(8,128)(2,1)}, bf16[512,2048]{1,0:T(8,128)(2,1)}, u32[]{:S(2)}, u32[]{:S(2)}) collective-permute-start(bf16[512,2048]{1,0:T(8,128)(2,1)} %shrink.1.refs_1_.refs_11_.refs_2_), channel_id=1, source_target_pairs={{0,1},{1,0},{2,3},{3,2},{4,5},{5,4},{6,7},{7,6},{8,9},{9,8},{10,11... | collective-permute-start | bytes 6291464 | tf_op jit(solution)/shard_map/ppermute | solution.py:989
  110.8 51.4 %collective-permute-start.5 = (bf16[512,2048]{1,0:T(8,128)(2,1)}, bf16[512,2048]{1,0:T(8,128)(2,1)}, u32[]{:S(2)}, u32[]{:S(2)}) collective-permute-start(bf16[512,2048]{1,0:T(8,128)(2,1)} %shrink.1.refs_1_.refs_11_.refs_2_), channel_id=1, source_target_pairs={{0,2},{1,3},{2,0},{3,1},{4,6},{5,7},{6,4},{7,5},{8,10},{9,11},{10,... | collective-permute-start | bytes 6291464 | tf_op jit(solution)/shard_map/ppermute | solution.py:989
  153.2 69.8 %collective-permute-start.9 = (bf16[256,2048]{1,0:T(8,128)(2,1)S(1)}, bf16[256,2048]{1,0:T(8,128)(2,1)S(1)}, u32[]{:S(2)}, u32[]{:S(2)}) collective-permute-start(bf16[256,2048]{1,0:T(8,128)(2,1)S(1)} %get-tuple-element.182), channel_id=1, source_target_pairs={{0,2},{1,3},{2,0},{3,1},{4,6},{5,7},{6,4},{7,5},{8,10},{9,11},{10,... | collective-permute-start | bytes 3145736 | tf_op jit(solution)/shard_map/ppermute | solution.py:989
  153.3 73.4 %collective-permute-start.7 = (bf16[256,2048]{1,0:T(8,128)(2,1)S(1)}, bf16[256,2048]{1,0:T(8,128)(2,1)S(1)}, u32[]{:S(2)}, u32[]{:S(2)}) collective-permute-start(bf16[256,2048]{1,0:T(8,128)(2,1)S(1)} %get-tuple-element.183), channel_id=1, source_target_pairs={{0,1},{1,0},{2,3},{3,2},{4,5},{5,4},{6,7},{7,6},{8,9},{9,8},{10,11... | collective-permute-start | bytes 3145736 | tf_op jit(solution)/shard_map/ppermute | solution.py:989
  224.3 47.3 %collective-permute-start.10 = (bf16[256,2048]{1,0:T(8,128)(2,1)}, bf16[256,2048]{1,0:T(8,128)(2,1)S(1)}, u32[]{:S(2)}, u32[]{:S(2)}) collective-permute-start(bf16[256,2048]{1,0:T(8,128)(2,1)} %fusion.7), channel_id=1, source_target_pairs={{0,1},{1,0},{2,3},{3,2},{4,5},{5,4},{6,7},{7,6},{8,9},{9,8},{10,11... | collective-permute-start | bytes 3145736 | tf_op jit(solution)/shard_map/ppermute | solution.py:989
  227.9 47.0 %collective-permute-start.8 = (bf16[256,2048]{1,0:T(8,128)(2,1)}, bf16[256,2048]{1,0:T(8,128)(2,1)S(1)}, u32[]{:S(2)}, u32[]{:S(2)}) collective-permute-start(bf16[256,2048]{1,0:T(8,128)(2,1)} %fusion.8), channel_id=1, source_target_pairs={{0,2},{1,3},{2,0},{3,1},{4,6},{5,7},{6,4},{7,5},{8,10},{9,11},{10,... | collective-permute-start | bytes 3145736 | tf_op jit(solution)/shard_map/ppermute | solution.py:989
  230.0 45.7 %collective-permute-start.11 = (bf16[256,2048]{1,0:T(8,128)(2,1)}, bf16[256,2048]{1,0:T(8,128)(2,1)S(1)}, u32[]{:S(2)}, u32[]{:S(2)}) collective-permute-start(bf16[256,2048]{1,0:T(8,128)(2,1)} %slice.139), channel_id=1, source_target_pairs={{0,2},{1,3},{2,0},{3,1},{4,6},{5,7},{6,4},{7,5},{8,10},{9,11},{10,... | collective-permute-start | bytes 3145736 | tf_op jit(solution)/shard_map/ppermute | solution.py:989
  230.1 45.7 %collective-permute-start.6 = (bf16[256,2048]{1,0:T(8,128)(2,1)S(1)}, bf16[256,2048]{1,0:T(8,128)(2,1)S(1)}, u32[]{:S(2)}, u32[]{:S(2)}) collective-permute-start(bf16[256,2048]{1,0:T(8,128)(2,1)S(1)} %slice.140), channel_id=1, source_target_pairs={{0,1},{1,0},{2,3},{3,2},{4,5},{5,4},{6,7},{7,6},{8,9},{9,8},{10,11... | collective-permute-start | bytes 3145736 | tf_op jit(solution)/shard_map/ppermute | solution.py:989
  248.7 49.6 %collective-permute-start.16 = (bf16[256,2048]{1,0:T(8,128)(2,1)}, bf16[256,2048]{1,0:T(8,128)(2,1)}, u32[]{:S(2)}, u32[]{:S(2)}) collective-permute-start(bf16[256,2048]{1,0:T(8,128)(2,1)} %get-tuple-element.117), channel_id=1, source_target_pairs={{0,2},{1,3},{2,0},{3,1},{4,6},{5,7},{6,4},{7,5},{8,10},{9,11},{10,... | collective-permute-start | bytes 3145736 | tf_op jit(solution)/shard_map/ppermute | solution.py:989
  285.0 42.1 %collective-permute-start.12 = (bf16[512,2048]{1,0:T(8,128)(2,1)}, bf16[512,2048]{1,0:T(8,128)(2,1)}, u32[]{:S(2)}, u32[]{:S(2)}) collective-permute-start(bf16[512,2048]{1,0:T(8,128)(2,1)} %get-tuple-element.113.refs_0_.refs_4_), channel_id=1, source_target_pairs={{0,1},{1,0},{2,3},{3,2},{4,5},{5,4},{6,7},{7,6},{8,9},{9,8},{10,11... | collective-permute-start | bytes 6291464 | tf_op jit(solution)/shard_map/ppermute | solution.py:989
  286.6 45.7 %collective-permute-start.13 = (bf16[512,2048]{1,0:T(8,128)(2,1)}, bf16[512,2048]{1,0:T(8,128)(2,1)}, u32[]{:S(2)}, u32[]{:S(2)}) collective-permute-start(bf16[512,2048]{1,0:T(8,128)(2,1)} %get-tuple-element.113.refs_0_.refs_4_), channel_id=1, source_target_pairs={{0,2},{1,3},{2,0},{3,1},{4,6},{5,7},{6,4},{7,5},{8,10},{9,11},{10,... | collective-permute-start | bytes 6291464 | tf_op jit(solution)/shard_map/ppermute | solution.py:989
  455.7 277.1 %reduce-scatter.8.cloned.1.call-start = ((), (), s32[]{:S(2)}) async-start(), calls=%async_computation.10 | async-start | bytes 3538944 | tf_op jit(solution)/shard_map/reduce_scatter | solution.py:1060
  461.4 37.5 %collective-permute-start.21 = (bf16[256,2048]{1,0:T(8,128)(2,1)S(1)}, bf16[256,2048]{1,0:T(8,128)(2,1)S(1)}, u32[]{:S(2)}, u32[]{:S(2)}) collective-permute-start(bf16[256,2048]{1,0:T(8,128)(2,1)S(1)} %copy-done.24), channel_id=1, source_target_pairs={{0,2},{1,3},{2,0},{3,1},{4,6},{5,7},{6,4},{7,5},{8,10},{9,11},{10,... | collective-permute-start | bytes 3145736 | tf_op jit(solution)/shard_map/ppermute | solution.py:989
  462.0 36.9 %collective-permute-start.22 = (bf16[256,2048]{1,0:T(8,128)(2,1)S(1)}, bf16[256,2048]{1,0:T(8,128)(2,1)}, u32[]{:S(2)}, u32[]{:S(2)}) collective-permute-start(bf16[256,2048]{1,0:T(8,128)(2,1)S(1)} %copy-done.26), channel_id=1, source_target_pairs={{0,1},{1,0},{2,3},{3,2},{4,5},{5,4},{6,7},{7,6},{8,9},{9,8},{10,11... | collective-permute-start | bytes 3145736 | tf_op jit(solution)/shard_map/ppermute | solution.py:989
  510.4 39.0 %collective-permute-start.24 = (bf16[512,2048]{1,0:T(8,128)(2,1)}, bf16[512,2048]{1,0:T(8,128)(2,1)}, u32[]{:S(2)}, u32[]{:S(2)}) collective-permute-start(bf16[512,2048]{1,0:T(8,128)(2,1)} %get-tuple-element.135.refs_0_.refs_5_), channel_id=1, source_target_pairs={{0,1},{1,0},{2,3},{3,2},{4,5},{5,4},{6,7},{7,6},{8,9},{9,8},{10,11... | collective-permute-start | bytes 6291464 | tf_op jit(solution)/shard_map/ppermute | solution.py:989
  512.6 36.8 %collective-permute-start.25 = (bf16[512,2048]{1,0:T(8,128)(2,1)}, bf16[512,2048]{1,0:T(8,128)(2,1)}, u32[]{:S(2)}, u32[]{:S(2)}) collective-permute-start(bf16[512,2048]{1,0:T(8,128)(2,1)} %get-tuple-element.135.refs_0_.refs_5_), channel_id=1, source_target_pairs={{0,2},{1,3},{2,0},{3,1},{4,6},{5,7},{6,4},{7,5},{8,10},{9,11},{10,... | collective-permute-start | bytes 6291464 | tf_op jit(solution)/shard_map/ppermute | solution.py:989
  659.2 174.5 %reduce-scatter.12.cloned.1.call-start = ((), (), s32[]{:S(2)}) async-start(), calls=%async_computation.12 | async-start | bytes 2359296 | tf_op jit(solution)/shard_map/reduce_scatter | solution.py:1060
  670.5 167.0 %reduce-scatter.14.cloned.1.call-start = ((), (), s32[]{:S(2)}) async-start(), calls=%async_computation.13 | async-start | bytes 6488064 | tf_op jit(solution)/shard_map/reduce_scatter | solution.py:1060
  671.2 174.1 %reduce-scatter.10.cloned.1.call-start = ((), (), s32[]{:S(2)}) async-start(), calls=%async_computation.11 | async-start | bytes 3538944 | tf_op jit(solution)/shard_map/reduce_scatter | solution.py:1060
  671.3 61.4 %collective-permute-start.30 = (bf16[256,2048]{1,0:T(8,128)(2,1)}, bf16[256,2048]{1,0:T(8,128)(2,1)S(1)}, u32[]{:S(2)}, u32[]{:S(2)}) collective-permute-start(bf16[256,2048]{1,0:T(8,128)(2,1)} %get-tuple-element.145), channel_id=1, source_target_pairs={{0,1},{1,0},{2,3},{3,2},{4,5},{5,4},{6,7},{7,6},{8,9},{9,8},{10,11... | collective-permute-start | bytes 3145736 | tf_op jit(solution)/shard_map/ppermute | solution.py:989
  671.8 60.9 %collective-permute-start.33 = (bf16[256,2048]{1,0:T(8,128)(2,1)}, bf16[256,2048]{1,0:T(8,128)(2,1)}, u32[]{:S(2)}, u32[]{:S(2)}) collective-permute-start(bf16[256,2048]{1,0:T(8,128)(2,1)} %get-tuple-element.146), channel_id=1, source_target_pairs={{0,2},{1,3},{2,0},{3,1},{4,6},{5,7},{6,4},{7,5},{8,10},{9,11},{10,... | collective-permute-start | bytes 3145736 | tf_op jit(solution)/shard_map/ppermute | solution.py:989
  675.3 57.5 %collective-permute-start.32 = (bf16[256,2048]{1,0:T(8,128)(2,1)S(1)}, bf16[256,2048]{1,0:T(8,128)(2,1)}, u32[]{:S(2)}, u32[]{:S(2)}) collective-permute-start(bf16[256,2048]{1,0:T(8,128)(2,1)S(1)} %add_convert_fusion.2.refs_2_), channel_id=1, source_target_pairs={{0,1},{1,0},{2,3},{3,2},{4,5},{5,4},{6,7},{7,6},{8,9},{9,8},{10,11... | collective-permute-start | bytes 3145736 | tf_op jit(solution)/shard_map/ppermute | solution.py:989
  678.8 54.0 %collective-permute-start.31 = (bf16[256,2048]{1,0:T(8,128)(2,1)S(1)}, bf16[256,2048]{1,0:T(8,128)(2,1)S(1)}, u32[]{:S(2)}, u32[]{:S(2)}) collective-permute-start(bf16[256,2048]{1,0:T(8,128)(2,1)S(1)} %add_convert_fusion.3.refs_3_), channel_id=1, source_target_pairs={{0,2},{1,3},{2,0},{3,1},{4,6},{5,7},{6,4},{7,5},{8,10},{9,11},{10,... | collective-permute-start | bytes 3145736 | tf_op jit(solution)/shard_map/ppermute | solution.py:989
  770.4 40.8 %collective-permute-start.34 = (bf16[256,2048]{1,0:T(8,128)(2,1)}, bf16[256,2048]{1,0:T(8,128)(2,1)S(1)}, u32[]{:S(2)}, u32[]{:S(2)}) collective-permute-start(bf16[256,2048]{1,0:T(8,128)(2,1)} %slice.103), channel_id=1, source_target_pairs={{0,1},{1,0},{2,3},{3,2},{4,5},{5,4},{6,7},{7,6},{8,9},{9,8},{10,11... | collective-permute-start | bytes 3145736 | tf_op jit(solution)/shard_map/ppermute | solution.py:989
  773.2 38.0 %collective-permute-start.39 = (bf16[256,2048]{1,0:T(8,128)(2,1)}, bf16[256,2048]{1,0:T(8,128)(2,1)}, u32[]{:S(2)}, u32[]{:S(2)}) collective-permute-start(bf16[256,2048]{1,0:T(8,128)(2,1)} %slice.108), channel_id=1, source_target_pairs={{0,2},{1,3},{2,0},{3,1},{4,6},{5,7},{6,4},{7,5},{8,10},{9,11},{10,... | collective-permute-start | bytes 3145736 | tf_op jit(solution)/shard_map/ppermute | solution.py:989
  (83 other events, 810.5 us)
Sparse Core Ops, SparseCore 0:
  10.2 67.4 all-gather.4
  79.8 29.5 all-gather.6
  111.0 59.9 all-gather.10
  173.0 106.2 all-gather.8
  455.9 118.7 reduce-scatter.5
  659.3 37.8 reduce-scatter.7
  699.5 34.8 reduce-scatter.11
  736.7 63.3 reduce-scatter.13
  802.4 41.5 reduce-scatter.9
